TPU v7x, 32 devices: a whole 2x2x4 slice. The times are simulated.
32 devices in a mesh: section: 2 (over core), dp: 4 (over z), tensor: 4 (over y, x).
Axes of the slice: x: 2, y: 2, z: 4, core: 2. Of those that a mesh axis runs over, the one named last changes fastest.
Arguments:
- states: bfloat16 [2, 4096, 1024], P(None, ('dp', 'tensor')), may hold values from -6 to 6
- segment_ids: int32 [2, 4096], P(None, 'dp'), may hold values from 0 to 519, as said below
- cotangent: bfloat16 [2, 4096, 1024], P(None, ('dp', 'tensor')), may hold values from -6 to 6
- qkv_weight: bfloat16 [2, 1024, 3, 1024], P('section', None, None, 'tensor'), may hold values from -0.1875 to 0.1875
- out_weight: bfloat16 [2, 1024, 1024], P('section', 'tensor'), may hold values from -0.5 to 0.5
- up_weight: bfloat16 [2, 1024, 4096], P('section', None, 'tensor'), may hold values from -0.1875 to 0.1875
- up_bias: bfloat16 [2, 4096], P('section', 'tensor'), may hold values from -3 to 3
- down_weight: bfloat16 [2, 4096, 1024], P('section', 'tensor'), may hold values from -0.09375 to 0.09375
- norm_gain: bfloat16 [2, 2, 1024], P('section'), may hold values from 0.5 to 1.5
- shift_vec: bfloat16 [2, 4, 1024], P('section'), may hold values from -2 to 2
- prefix: bfloat16 [2, 2, 64, 1024], P('section', None, None, 'tensor'), may hold values from -6 to 6
Outputs:
- hidden_out: bfloat16 [2, 2, 4096, 1024], P('section', None, ('dp', 'tensor'))
- input_grads: float32 [2, 2, 4096, 1024], P('section', None, ('dp', 'tensor'))
- prefix_grads: float32 [2, 2, 64, 1024], P('section', None, None, 'tensor')
Inputs may be any that keep to these rules, and one draw needn't show every extreme that they name: `segment_ids`: segment numbers never fall along a micro-batch; every sequence of 1024 tokens starts a new segment, so sequences share none; in every sequence one segment covers all of it but at most 32 tokens at each end. The k-th sequence of the whole batch (micro-batches in order) uses numbers from k * (65) to (k + 1) * 65 - 1, and its last token holds the highest of them.
All inputs are finite; a program needn't handle non-finite values.
Results may differ from a plain program's by a relative error of at most 0.03.
Values may be sent and summed in bfloat16 or wider, within the bound.
A program may use at most 192 MiB of HBM per device.

v0:
```python
import math

import jax
import jax.numpy as jnp
from jax import lax
from jax.sharding import PartitionSpec as P

D = 1024
HEAD = 64
PREFIX = 64
LEN = 1024
MICRO = 2
SEQS = 1


def from_behind(array, axis, by):
    size = lax.axis_size(axis)
    pairs = [(i, i + by) for i in range(size) if 0 <= i + by < size]
    return lax.ppermute(array, axis, pairs)


def rounded(values):
    return lax.optimization_barrier(values.astype(jnp.bfloat16)).astype(jnp.float32)


def norm_rows(values, gain, bias):
    center = values - jnp.mean(values, axis=-1, keepdims=True)
    spread = jnp.mean(center * center, axis=-1, keepdims=True)
    return center * lax.rsqrt(spread + 1e-05) * gain + bias


def along_rows(left_side, right_side):
    return lax.dot_general(
        left_side, right_side, (((1,), (1,)), ((), ())), preferred_element_type=jnp.float32
    )


def mask_scores(queries, keys_all, segment_query, segment_keys):
    scores = (
        jnp.einsum("qhe,khe->hqk", queries, keys_all, preferred_element_type=jnp.float32) * 0.125
    )
    visible = jnp.concatenate(
        [
            jnp.full((queries.shape[0], PREFIX), True),
            segment_query[:, None] == segment_keys[None, :],
        ],
        1,
    )
    return jnp.where(visible[None], scores, -1e30)


def attend(queries, keys_all, values_all, segment_query, segment_keys):
    block_size = math.gcd(queries.shape[0], 512)
    blocks = queries.shape[0] // block_size
    query_shape = queries.shape

    def block_fn(block_item):
        block_query, block_segment = block_item
        scores = mask_scores(block_query, keys_all, block_segment, segment_keys)
        peak_score = jnp.max(scores, axis=-1, keepdims=True)
        weights_exp = jnp.exp(scores - peak_score)
        normalizer = jnp.sum(weights_exp, axis=-1, keepdims=True)
        weights_soft = (weights_exp / normalizer).astype(jnp.bfloat16)
        result = jnp.einsum(
            "hqk,khe->qhe", weights_soft, values_all, preferred_element_type=jnp.float32
        )
        return (result.astype(jnp.bfloat16), (peak_score + jnp.log(normalizer))[..., 0])

    merged_heads, log_totals = lax.map(
        block_fn,
        (
            queries.reshape((blocks, block_size) + query_shape[1:]),
            segment_query.reshape(blocks, block_size),
        ),
    )
    return (merged_heads.reshape(query_shape), log_totals)


def attend_back(
    queries, keys_all, values_all, segment_query, segment_keys, log_totals, grad_merged
):
    block_size = math.gcd(queries.shape[0], 512)
    blocks = queries.shape[0] // block_size
    query_shape = queries.shape

    def block_fn(running, block_item):
        block_query, block_segment, block_totals, block_grad = block_item
        scores = mask_scores(block_query, keys_all, block_segment, segment_keys)
        weights_soft = jnp.exp(scores - block_totals[..., None])
        grad_soft = jnp.einsum(
            "qhe,khe->hqk", block_grad, values_all, preferred_element_type=jnp.float32
        )
        grad_scores = weights_soft * (
            grad_soft - jnp.sum(weights_soft * grad_soft, axis=-1, keepdims=True)
        )
        grad_scores = grad_scores.astype(jnp.bfloat16)
        grad_query = (
            jnp.einsum("hqk,khe->qhe", grad_scores, keys_all, preferred_element_type=jnp.float32)
            * 0.125
        )
        grad_keys = (
            running[0]
            + jnp.einsum(
                "hqk,qhe->khe", grad_scores, block_query, preferred_element_type=jnp.float32
            )
            * 0.125
        )
        grad_values = running[1] + jnp.einsum(
            "hqk,qhe->khe",
            weights_soft.astype(jnp.bfloat16),
            block_grad,
            preferred_element_type=jnp.float32,
        )
        return ((grad_keys, grad_values), grad_query.astype(jnp.bfloat16))

    zero_grads = jnp.zeros(keys_all.shape, jnp.float32)
    (grad_keys, grad_values), grad_query = lax.scan(
        block_fn,
        (zero_grads, zero_grads),
        (
            queries.reshape((blocks, block_size) + query_shape[1:]),
            segment_query.reshape(blocks, block_size),
            log_totals,
            grad_merged.reshape((blocks, block_size) + query_shape[1:]),
        ),
    )
    return (grad_query.reshape(query_shape), grad_keys, grad_values)


def forward_split(inputs, segment, weights):
    (
        query_key_value_matrix,
        output_matrix,
        up_matrix,
        up_offset_bias,
        down_matrix,
        gains,
        prefix_shifts,
        prefix_pair,
    ) = weights
    width = output_matrix.shape[0]
    heads = width // HEAD
    whole = jnp.dot(
        lax.all_gather(inputs.astype(jnp.bfloat16), "tensor", axis=0, tiled=True),
        query_key_value_matrix,
        preferred_element_type=jnp.float32,
    )
    projected_rows = whole.astype(jnp.bfloat16).reshape(SEQS, LEN, 3, heads, HEAD)
    keys_pre = prefix_pair[0].reshape(PREFIX, heads, HEAD)
    values_pre = prefix_pair[1].reshape(PREFIX, heads, HEAD)

    def forward_one_sequence(sequence_item):
        queries, keys_seq, values_seq, segment_one = sequence_item
        return attend(
            queries,
            jnp.concatenate([keys_pre, keys_seq], 0),
            jnp.concatenate([values_pre, values_seq], 0),
            segment_one,
            segment_one,
        )

    merged_heads, log_totals = lax.map(
        forward_one_sequence,
        (
            projected_rows[:, :, 0],
            projected_rows[:, :, 1],
            projected_rows[:, :, 2],
            segment.reshape(SEQS, LEN),
        ),
    )
    merged_heads = merged_heads.reshape(SEQS * LEN, width)
    attended_rows = (
        lax.psum_scatter(
            jnp.dot(merged_heads, output_matrix, preferred_element_type=jnp.float32).astype(
                jnp.bfloat16
            ),
            "tensor",
            scatter_dimension=0,
            tiled=True,
        ).astype(jnp.float32)
        + prefix_shifts[0]
    )
    middle = norm_rows(inputs + attended_rows, gains[0], prefix_shifts[1])
    hidden_state = (
        jnp.dot(
            lax.all_gather(middle.astype(jnp.bfloat16), "tensor", axis=0, tiled=True),
            up_matrix,
            preferred_element_type=jnp.float32,
        )
        + up_offset_bias
    )
    active_units = jax.nn.gelu(hidden_state, approximate=False).astype(jnp.bfloat16)
    branch_output = (
        lax.psum_scatter(
            jnp.dot(active_units, down_matrix, preferred_element_type=jnp.float32).astype(
                jnp.bfloat16
            ),
            "tensor",
            scatter_dimension=0,
            tiled=True,
        ).astype(jnp.float32)
        + prefix_shifts[2]
    )
    result = norm_rows(middle + branch_output, gains[1], prefix_shifts[3])
    return (
        result,
        (inputs, projected_rows, log_totals, attended_rows, middle, hidden_state, branch_output),
    )


def backward_split(grad_result, segment, weights, retained):
    (
        query_key_value_matrix,
        output_matrix,
        up_matrix,
        up_offset_bias,
        down_matrix,
        gains,
        prefix_shifts,
        prefix_pair,
    ) = weights
    inputs, projected_rows, log_totals, attended_rows, middle, hidden_state, branch_output = (
        retained
    )
    width = output_matrix.shape[0]
    heads = width // HEAD
    _, pull_last = jax.vjp(
        lambda resid: norm_rows(resid, gains[1], prefix_shifts[3]), middle + branch_output
    )
    (grad_second,) = pull_last(grad_result)
    grad_active = along_rows(
        lax.all_gather(grad_second.astype(jnp.bfloat16), "tensor", axis=0, tiled=True), down_matrix
    )
    _, pull_gelu = jax.vjp(
        lambda pre_active: jax.nn.gelu(pre_active, approximate=False), hidden_state
    )
    (grad_hidden,) = pull_gelu(grad_active)
    grad_hidden = grad_hidden.astype(jnp.bfloat16)
    grad_middle = lax.psum_scatter(
        along_rows(grad_hidden, up_matrix).astype(jnp.bfloat16),
        "tensor",
        scatter_dimension=0,
        tiled=True,
    ).astype(jnp.float32)
    grad_middle = grad_second + rounded(grad_middle)
    _, pull_first = jax.vjp(
        lambda resid: norm_rows(resid, gains[0], prefix_shifts[1]), inputs + attended_rows
    )
    (grad_first,) = pull_first(grad_middle)
    grad_merged = along_rows(
        lax.all_gather(grad_first.astype(jnp.bfloat16), "tensor", axis=0, tiled=True), output_matrix
    )
    grad_merged = grad_merged.astype(jnp.bfloat16).reshape(SEQS, LEN, heads, HEAD)
    keys_pre = prefix_pair[0].reshape(PREFIX, heads, HEAD)
    values_pre = prefix_pair[1].reshape(PREFIX, heads, HEAD)

    def backward_one_sequence(sequence_item):
        queries, keys_seq, values_seq, segment_one, totals_one, grad_one = sequence_item
        return attend_back(
            queries,
            jnp.concatenate([keys_pre, keys_seq], 0),
            jnp.concatenate([values_pre, values_seq], 0),
            segment_one,
            segment_one,
            totals_one,
            grad_one,
        )

    grad_query, grad_keys, grad_values = lax.map(
        backward_one_sequence,
        (
            projected_rows[:, :, 0],
            projected_rows[:, :, 1],
            projected_rows[:, :, 2],
            segment.reshape(SEQS, LEN),
            log_totals,
            grad_merged,
        ),
    )
    grad_projected = jnp.stack(
        [
            grad_query,
            grad_keys[:, PREFIX:].astype(jnp.bfloat16),
            grad_values[:, PREFIX:].astype(jnp.bfloat16),
        ],
        2,
    ).reshape(SEQS * LEN, 3 * width)
    grad_inputs = lax.psum_scatter(
        along_rows(grad_projected, query_key_value_matrix).astype(jnp.bfloat16),
        "tensor",
        scatter_dimension=0,
        tiled=True,
    ).astype(jnp.float32)
    grad_inputs = grad_first + rounded(grad_inputs)
    prefix_term = jnp.stack(
        [jnp.sum(grad_keys[:, :PREFIX], 0), jnp.sum(grad_values[:, :PREFIX], 0)]
    ).reshape(2, PREFIX, width)
    return (grad_inputs, prefix_term)


def local(
    states,
    segment_ids,
    cotangent,
    qkv_weight,
    out_weight,
    up_weight,
    up_bias,
    down_weight,
    norm_gain,
    shift_vec,
    prefix,
):
    section_first = lax.axis_index("section") == 0
    gains = norm_gain[0].astype(jnp.float32)
    prefix_shifts = shift_vec[0].astype(jnp.float32)
    weights = (
        qkv_weight[0].reshape(D, -1),
        out_weight[0],
        up_weight[0],
        up_bias[0].astype(jnp.float32),
        down_weight[0],
        gains,
        prefix_shifts,
        prefix[0],
    )
    incoming = jnp.zeros(states.shape[1:], jnp.bfloat16)
    section_inputs, section_segments, retained_steps, results = ([], [], [], [])
    for moment in range(MICRO + 1):
        inputs = jnp.where(section_first, states[min(moment, MICRO - 1)], incoming).astype(
            jnp.float32
        )
        segment = jnp.where(
            section_first, segment_ids[min(moment, MICRO - 1)], segment_ids[max(moment - 1, 0)]
        )
        result, retained = forward_split(inputs, segment, weights)
        result = result.astype(jnp.bfloat16)
        if moment < MICRO:
            incoming = from_behind(result, "section", 1)
        section_inputs.append(inputs)
        section_segments.append(segment)
        results.append(result)
    arriving = jnp.zeros(states.shape[1:], jnp.bfloat16)
    grads_steps = []
    prefix_sum = None
    for moment in range(MICRO + 1):
        index_back = MICRO - moment
        grad_result = jnp.where(
            section_first, arriving, cotangent[max(MICRO - 1 - moment, 0)]
        ).astype(jnp.float32)
        _, retained = forward_split(
            section_inputs[index_back], section_segments[index_back], weights
        )
        grad_inputs, prefix_term = backward_split(
            grad_result, section_segments[index_back], weights, retained
        )
        useful = jnp.where(section_first, moment >= 1, moment <= MICRO - 1)
        prefix_term = jnp.where(useful, prefix_term, 0.0)
        prefix_sum = prefix_term if prefix_sum is None else prefix_sum + prefix_term
        if moment < MICRO:
            arriving = from_behind(grad_inputs.astype(jnp.bfloat16), "section", -1)
        grads_steps.append(grad_inputs)
    prefix_grads = lax.psum(prefix_sum.astype(jnp.bfloat16), "dp").astype(jnp.float32)
    hidden_out = jnp.stack(
        [
            jnp.where(section_first, results[micro_index], results[micro_index + 1])
            for micro_index in range(MICRO)
        ]
    )
    input_grads = jnp.stack(
        [
            jnp.where(
                section_first,
                grads_steps[MICRO - micro_index],
                grads_steps[MICRO - 1 - micro_index],
            )
            for micro_index in range(MICRO)
        ]
    )
    return (hidden_out[None], input_grads[None], prefix_grads[None])


def solution(mesh):
    placed = (
        P(None, ("dp", "tensor"), None),
        P(None, "dp"),
        P(None, ("dp", "tensor"), None),
        P("section", None, None, "tensor"),
        P("section", "tensor", None),
        P("section", None, "tensor"),
        P("section", "tensor"),
        P("section", "tensor", None),
        P("section", None, None),
        P("section", None, None),
        P("section", None, None, "tensor"),
    )
    return jax.shard_map(
        local,
        mesh=mesh,
        in_specs=placed,
        out_specs=(
            P("section", None, ("dp", "tensor"), None),
            P("section", None, ("dp", "tensor"), None),
            P("section", None, None, "tensor"),
        ),
        check_vma=False,
    )
```

profile of v0, /device:TPU:0, one launch (start us, length us, event | category | flops | bytes accessed | tf_op | source)
XLA Modules:
  0.0 1738.4 jit_solution(12777574989585157310)
XLA Ops:
  13.4 35.1 %all-gather.45.cloned.1.call-done = bf16[1,1024,1024]{2,1,0:T(8,128)(2,1)} async-done(((bf16[1,256,1024]{2,1,0:T(8,128)(2,1)}), bf16[1,1024,1024]{2,1,0:T(8,128)(2,1)}) %all-gather.45.cloned.1.call-update) | async-done | bytes 2097168 | tf_op jit(solution)/shard_map/all_gather | solution.py:144
  57.4 15.2 while.197
  78.5 24.3 %while.192 = (s32[]{:T(128)}, bf16[2,512,4,64]{1,3,2,0:T(8,128)(2,1)}, s32[2,512]{1,0:T(2,128)S(1)}, s32[1024]{0:T(1024)S(1)}, bf16[2,512,4,64]{1,3,2,0:T(8,128)...) while((s32[]{:T(128)}, ...), condition=%wide.region_3.4_spmd, body=%wide.region_0.3_spmd.sunk | while | flops 876351616 | bytes 5303398 | solution.py:69
  84.2 6.4 fusion.783
  96.4 6.5 fusion.783
  112.7 38.5 %reduce-scatter.19.cloned.1.call-done = bf16[256,1024]{1,0:T(8,128)(2,1)} async-done(((bf16[1024,1024]{1,0:T(8,128)(2,1)}), bf16[256,1024]{1,0:T(8,128)(2,1)}) %reduce-scatter.19.cloned.1.call-update) | async-done | bytes 524304 | tf_op jit(solution)/shard_map/reduce_scatter | solution.py:173
  159.0 34.4 %all-gather.39.cloned.1.call-done = bf16[1024,1024]{1,0:T(8,128)(2,1)} async-done(((bf16[256,1024]{1,0:T(8,128)(2,1)}), bf16[1024,1024]{1,0:T(8,128)(2,1)}) %all-gather.39.cloned.1.call-update) | async-done | bytes 2097168 | tf_op jit(solution)/shard_map/all_gather | solution.py:186
  193.4 12.4 fusion.236
  212.9 17.6 %all-gather.17.cloned.1.call-done = bf16[1024,1024]{1,0:T(8,128)(2,1)} async-done(((bf16[256,1024]{1,0:T(8,128)(2,1)}), bf16[1024,1024]{1,0:T(8,128)(2,1)}) %all-gather.17.cloned.1.call-update) | async-done | bytes 2097168 | tf_op jit(solution)/shard_map/all_gather | solution.py:186
  230.4 15.5 fusion.434
  246.2 22.8 %reduce-scatter.49.cloned.1.call-done = bf16[256,1024]{1,0:T(8,128)(2,1)} async-done(((bf16[1024,1024]{1,0:T(8,128)(2,1)}), bf16[256,1024]{1,0:T(8,128)(2,1)}) %reduce-scatter.49.cloned.1.call-update) | async-done | bytes 524304 | tf_op jit(solution)/shard_map/reduce_scatter | solution.py:194
  269.1 38.5 %reduce-scatter.21.cloned.1.call-done = bf16[256,1024]{1,0:T(8,128)(2,1)} async-done(((bf16[1024,1024]{1,0:T(8,128)(2,1)}), bf16[256,1024]{1,0:T(8,128)(2,1)}) %reduce-scatter.21.cloned.1.call-update) | async-done | bytes 524304 | tf_op jit(solution)/shard_map/reduce_scatter | solution.py:194
  317.2 35.3 %all-gather.19.cloned.1.call-done = bf16[1024,1024]{1,0:T(8,128)(2,1)} async-done(((bf16[256,1024]{1,0:T(8,128)(2,1)}), bf16[1024,1024]{1,0:T(8,128)(2,1)}) %all-gather.19.cloned.1.call-update) | async-done | bytes 2097168 | tf_op jit(solution)/shard_map/all_gather | solution.py:144
  363.1 19.2 %while.196 = (s32[]{:T(128)}, bf16[2,512,4,64]{1,3,2,0:T(8,128)(2,1)}, f32[2,4,512]{2,1,0:T(4,128)S(1)}, s32[2,512]{1,0:T(2,128)S(1)}, s32[1024]{0:T(1024)S(1)},...) while((s32[]{:T(128)}, ...), condition=%wide.region_52.53_spmd, body=%wide.region_49.52_spmd.sunk | while | flops 597817344 | bytes 31763564 | solution.py:69
  387.1 22.6 %while.193 = (s32[]{:T(128)}, bf16[2,512,4,64]{1,3,2,0:T(8,128)(2,1)}, s32[2,512]{1,0:T(2,128)S(1)}, s32[1024]{0:T(1024)S(1)}, bf16[2,512,4,64]{1,3,2,0:T(8,128)...) while((s32[]{:T(128)}, ...), condition=%wide.region_13.14_spmd, body=%wide.region_10.13_spmd.sunk | while | flops 876351616 | bytes 5238370 | solution.py:69
  392.0 6.5 fusion.790
  422.7 37.0 %reduce-scatter.23.cloned.1.call-done = bf16[256,1024]{1,0:T(8,128)(2,1)} async-done(((bf16[1024,1024]{1,0:T(8,128)(2,1)}), bf16[256,1024]{1,0:T(8,128)(2,1)}) %reduce-scatter.23.cloned.1.call-update) | async-done | bytes 524304 | tf_op jit(solution)/shard_map/reduce_scatter | solution.py:173
  466.7 34.4 %all-gather.33.cloned.1.call-done = bf16[1024,1024]{1,0:T(8,128)(2,1)} async-done(((bf16[256,1024]{1,0:T(8,128)(2,1)}), bf16[1024,1024]{1,0:T(8,128)(2,1)}) %all-gather.33.cloned.1.call-update) | async-done | bytes 2097168 | tf_op jit(solution)/shard_map/all_gather | solution.py:186
  501.1 12.3 fusion.235
  520.5 17.6 %all-gather.21.cloned.1.call-done = bf16[1024,1024]{1,0:T(8,128)(2,1)} async-done(((bf16[256,1024]{1,0:T(8,128)(2,1)}), bf16[1024,1024]{1,0:T(8,128)(2,1)}) %all-gather.21.cloned.1.call-update) | async-done | bytes 2097168 | tf_op jit(solution)/shard_map/all_gather | solution.py:186
  538.1 15.5 fusion.439
  553.9 23.0 %reduce-scatter.41.cloned.1.call-done = bf16[256,1024]{1,0:T(8,128)(2,1)} async-done(((bf16[1024,1024]{1,0:T(8,128)(2,1)}), bf16[256,1024]{1,0:T(8,128)(2,1)}) %reduce-scatter.41.cloned.1.call-update) | async-done | bytes 524304 | tf_op jit(solution)/shard_map/reduce_scatter | solution.py:194
  576.9 38.3 %reduce-scatter.25.cloned.1.call-done = bf16[256,1024]{1,0:T(8,128)(2,1)} async-done(((bf16[1024,1024]{1,0:T(8,128)(2,1)}), bf16[256,1024]{1,0:T(8,128)(2,1)}) %reduce-scatter.25.cloned.1.call-update) | async-done | bytes 524304 | tf_op jit(solution)/shard_map/reduce_scatter | solution.py:194
  625.8 35.4 %all-gather.23.cloned.1.call-done = bf16[1024,1024]{1,0:T(8,128)(2,1)} async-done(((bf16[256,1024]{1,0:T(8,128)(2,1)}), bf16[1024,1024]{1,0:T(8,128)(2,1)}) %all-gather.23.cloned.1.call-update) | async-done | bytes 2097168 | tf_op jit(solution)/shard_map/all_gather | solution.py:144
  671.8 19.2 %while.195 = (s32[]{:T(128)}, bf16[2,512,4,64]{1,3,2,0:T(8,128)(2,1)}, f32[2,4,512]{2,1,0:T(4,128)S(1)}, s32[2,512]{1,0:T(2,128)S(1)}, s32[1024]{0:T(1024)S(1)},...) while((s32[]{:T(128)}, ...), condition=%wide.region_33.34_spmd, body=%wide.region_30.33_spmd.sunk | while | flops 597817344 | bytes 31763564 | solution.py:69
  696.1 35.1 %reduce-scatter.31.cloned.1.call-done = bf16[256,1024]{1,0:T(8,128)(2,1)} async-done(((bf16[1024,1024]{1,0:T(8,128)(2,1)}), bf16[256,1024]{1,0:T(8,128)(2,1)}) %reduce-scatter.31.cloned.1.call-update) | async-done | bytes 524304 | tf_op jit(solution)/shard_map/reduce_scatter | solution.py:173
  736.1 35.4 %all-gather.27.cloned.1.call-done = bf16[1024,1024]{1,0:T(8,128)(2,1)} async-done(((bf16[256,1024]{1,0:T(8,128)(2,1)}), bf16[1024,1024]{1,0:T(8,128)(2,1)}) %all-gather.27.cloned.1.call-update) | async-done | bytes 2097168 | tf_op jit(solution)/shard_map/all_gather | solution.py:186
  771.5 12.4 fusion.234
  790.9 35.3 %reduce-scatter.33.cloned.1.call-done = bf16[256,1024]{1,0:T(8,128)(2,1)} async-done(((bf16[1024,1024]{1,0:T(8,128)(2,1)}), bf16[256,1024]{1,0:T(8,128)(2,1)}) %reduce-scatter.33.cloned.1.call-update) | async-done | bytes 524304 | tf_op jit(solution)/shard_map/reduce_scatter | solution.py:194
  832.0 35.4 %all-gather.29.cloned.1.call-done = bf16[1024,1024]{1,0:T(8,128)(2,1)} async-done(((bf16[256,1024]{1,0:T(8,128)(2,1)}), bf16[1024,1024]{1,0:T(8,128)(2,1)}) %all-gather.29.cloned.1.call-update) | async-done | bytes 2097168 | tf_op jit(solution)/shard_map/all_gather | solution.py:232
  867.4 10.7 fusion.416
  879.4 24.8 %while.194 = (s32[]{:T(128)}, bf16[2,512,4,64]{1,3,2,0:T(8,128)(2,1)}, s32[2,512]{1,0:T(2,128)S(1)}, s32[1024]{0:T(1024)S(1)}, bf16[2,512,4,64]{1,3,2,0:T(8,128)...) while((s32[]{:T(128)}, ...), condition=%wide.region_23.24_spmd, body=%wide.region_20.23_spmd.sunk | while | flops 876351616 | bytes 5238370 | solution.py:69
  885.3 6.5 fusion.797
  897.8 6.5 fusion.797
  913.5 38.5 %reduce-scatter.27.cloned.1.call-done = bf16[256,1024]{1,0:T(8,128)(2,1)} async-done(((bf16[1024,1024]{1,0:T(8,128)(2,1)}), bf16[256,1024]{1,0:T(8,128)(2,1)}) %reduce-scatter.27.cloned.1.call-update) | async-done | bytes 524304 | tf_op jit(solution)/shard_map/reduce_scatter | solution.py:173
  959.4 35.2 %all-gather.31.cloned.1.call-done = bf16[1024,1024]{1,0:T(8,128)(2,1)} async-done(((bf16[256,1024]{1,0:T(8,128)(2,1)}), bf16[1024,1024]{1,0:T(8,128)(2,1)}) %all-gather.31.cloned.1.call-update) | async-done | bytes 2097168 | tf_op jit(solution)/shard_map/all_gather | solution.py:251
  1000.8 64.0 %while.198 = (s32[]{:T(128)}, f32[1088,4,64]{0,2,1:T(8,128)}, f32[1088,4,64]{0,2,1:T(8,128)}, bf16[2,512,4,64]{1,3,2,0:T(8,128)(2,1)}, bf16[2,512,4,64]{1,3,2,0:...) while((s32[]{:T(128)}, f32[1088,4,64]{0,2,1:T(8,128)}, ...), condition=%wide.region_47.48_spmd.clone, body=%wide.region_45.47_spmd.clone.sunk | while | flops 1448294400 | bytes 170052992 | solution.py:117
  1003.9 8.0 multiply_reduce_fusion.23
  1011.8 10.6 multiply_convert_fusion.18
  1035.0 8.0 multiply_reduce_fusion.23
  1042.9 10.6 multiply_convert_fusion.18
  1073.3 35.3 %reduce-scatter.37.cloned.1.call-done = bf16[256,1024]{1,0:T(8,128)(2,1)} async-done(((bf16[1024,1024]{1,0:T(8,128)(2,1)}), bf16[256,1024]{1,0:T(8,128)(2,1)}) %reduce-scatter.37.cloned.1.call-update) | async-done | bytes 524304 | tf_op jit(solution)/shard_map/reduce_scatter | solution.py:288
  1118.2 35.4 %all-gather.35.cloned.1.call-done = bf16[1024,1024]{1,0:T(8,128)(2,1)} async-done(((bf16[256,1024]{1,0:T(8,128)(2,1)}), bf16[1024,1024]{1,0:T(8,128)(2,1)}) %all-gather.35.cloned.1.call-update) | async-done | bytes 2097168 | tf_op jit(solution)/shard_map/all_gather | solution.py:232
  1153.6 10.7 fusion.419
  1164.4 35.3 %reduce-scatter.43.cloned.1.call-done = bf16[256,1024]{1,0:T(8,128)(2,1)} async-done(((bf16[1024,1024]{1,0:T(8,128)(2,1)}), bf16[256,1024]{1,0:T(8,128)(2,1)}) %reduce-scatter.43.cloned.1.call-update) | async-done | bytes 524304 | tf_op jit(solution)/shard_map/reduce_scatter | solution.py:239
  1205.7 35.4 %all-gather.37.cloned.1.call-done = bf16[1024,1024]{1,0:T(8,128)(2,1)} async-done(((bf16[256,1024]{1,0:T(8,128)(2,1)}), bf16[1024,1024]{1,0:T(8,128)(2,1)}) %all-gather.37.cloned.1.call-update) | async-done | bytes 2097168 | tf_op jit(solution)/shard_map/all_gather | solution.py:251
  1247.7 63.9 %while.199 = (s32[]{:T(128)}, f32[1088,4,64]{0,2,1:T(8,128)}, f32[1088,4,64]{0,2,1:T(8,128)}, bf16[2,512,4,64]{1,3,2,0:T(8,128)(2,1)}, bf16[2,512,4,64]{1,3,2,0:...) while((s32[]{:T(128)}, f32[1088,4,64]{0,2,1:T(8,128)}, ...), condition=%wide.region_66.67_spmd.clone, body=%wide.region_64.66_spmd.clone.sunk | while | flops 1448294400 | bytes 169921856 | solution.py:117
  1250.7 8.0 multiply_reduce_fusion.24
  1258.7 10.6 multiply_convert_fusion.19
  1281.7 7.9 multiply_reduce_fusion.24
  1289.7 10.6 multiply_convert_fusion.19
  1320.0 35.3 %reduce-scatter.45.cloned.1.call-done = bf16[256,1024]{1,0:T(8,128)(2,1)} async-done(((bf16[1024,1024]{1,0:T(8,128)(2,1)}), bf16[256,1024]{1,0:T(8,128)(2,1)}) %reduce-scatter.45.cloned.1.call-update) | async-done | bytes 524304 | tf_op jit(solution)/shard_map/reduce_scatter | solution.py:288
  1364.9 35.4 %all-gather.41.cloned.1.call-done = bf16[1024,1024]{1,0:T(8,128)(2,1)} async-done(((bf16[256,1024]{1,0:T(8,128)(2,1)}), bf16[1024,1024]{1,0:T(8,128)(2,1)}) %all-gather.41.cloned.1.call-update) | async-done | bytes 2097168 | tf_op jit(solution)/shard_map/all_gather | solution.py:232
  1400.3 10.7 fusion.422
  1411.1 35.3 %reduce-scatter.51.cloned.1.call-done = bf16[256,1024]{1,0:T(8,128)(2,1)} async-done(((bf16[1024,1024]{1,0:T(8,128)(2,1)}), bf16[256,1024]{1,0:T(8,128)(2,1)}) %reduce-scatter.51.cloned.1.call-update) | async-done | bytes 524304 | tf_op jit(solution)/shard_map/reduce_scatter | solution.py:239
  1451.1 35.4 %all-gather.25.cloned.1.call-done = bf16[1024,1024]{1,0:T(8,128)(2,1)} async-done(((bf16[256,1024]{1,0:T(8,128)(2,1)}), bf16[1024,1024]{1,0:T(8,128)(2,1)}) %all-gather.25.cloned.1.call-update) | async-done | bytes 2097168 | tf_op jit(solution)/shard_map/all_gather | solution.py:186
  1486.5 15.7 fusion.444
  1502.3 35.3 %reduce-scatter.29.cloned.1.call-done = bf16[256,1024]{1,0:T(8,128)(2,1)} async-done(((bf16[1024,1024]{1,0:T(8,128)(2,1)}), bf16[256,1024]{1,0:T(8,128)(2,1)}) %reduce-scatter.29.cloned.1.call-update) | async-done | bytes 524304 | tf_op jit(solution)/shard_map/reduce_scatter | solution.py:194
  1547.5 31.3 %all-gather.43.cloned.1.call-done = bf16[1024,1024]{1,0:T(8,128)(2,1)} async-done(((bf16[256,1024]{1,0:T(8,128)(2,1)}), bf16[1024,1024]{1,0:T(8,128)(2,1)}) %all-gather.43.cloned.1.call-update) | async-done | bytes 2097168 | tf_op jit(solution)/shard_map/all_gather | solution.py:251
  1588.2 59.9 %while.200 = (s32[]{:T(128)}, f32[1088,4,64]{0,2,1:T(8,128)}, f32[1088,4,64]{0,2,1:T(8,128)}, bf16[2,512,4,64]{1,3,2,0:T(8,128)(2,1)}, bf16[2,512,4,64]{1,3,2,0:...) while((s32[]{:T(128)}, f32[1088,4,64]{0,2,1:T(8,128)}, ...), condition=%wide.region_85.86_spmd.clone, body=%wide.region_83.85_spmd.clone.sunk | while | flops 1448294400 | bytes 172018528 | solution.py:117
  1596.9 10.6 multiply_convert_fusion.20
  1626.1 10.6 multiply_convert_fusion.20
  1669.1 19.6 %all-reduce.11.cloned.1.call-done = bf16[1,2,64,256]{3,2,1,0:T(8,128)(2,1)} async-done(((bf16[1,2,64,256]{3,2,1,0:T(8,128)(2,1)}), bf16[1,2,64,256]{3,2,1,0:T(8,128)(2,1)}) %all-reduce.11.cloned.1.call-update) | async-done | bytes 65552 | tf_op jit(solution)/shard_map/psum | solution.py:363
  1690.2 37.0 %reduce-scatter.53.cloned.1.call-done = bf16[256,1024]{1,0:T(8,128)(2,1)} async-done(((bf16[1024,1024]{1,0:T(8,128)(2,1)}), bf16[256,1024]{1,0:T(8,128)(2,1)}) %reduce-scatter.53.cloned.1.call-update) | async-done | bytes 524304 | tf_op jit(solution)/shard_map/reduce_scatter | solution.py:288
  (692 shorter events, 447.9 us)
Async XLA Ops:
  7.2 186.2 %copy-start = (bf16[1,1024,1024]{2,1,0:T(8,128)(2,1)S(1)}, bf16[1,1024,1024]{2,1,0:T(8,128)(2,1)}, u32[]{:S(2)}) copy-start(bf16[1,1024,1024]{2,1,0:T(8,128)(2,1)} %param.34) | copy-start | bytes 6291460
  7.2 41.3 %all-gather.45.cloned.1.call-start = ((), (), s32[]{:S(2)}) async-start(), calls=%async_computation.51 | async-start | bytes 2621440 | tf_op jit(solution)/shard_map/all_gather | solution.py:144
  9.3 103.4 %reduce-scatter.47.cloned.1.call-start = ((), (), s32[]{:S(2)}) async-start(), calls=%async_computation.43 | async-start | bytes 2621440 | tf_op jit(solution)/shard_map/reduce_scatter | solution.py:173
  77.4 73.8 %reduce-scatter.19.cloned.1.call-start = ((), (), s32[]{:S(2)}) async-start(), calls=%async_computation.18 | async-start | bytes 2621440 | tf_op jit(solution)/shard_map/reduce_scatter | solution.py:173
  102.8 214.2 %copy-start.73 = (s32[2,512]{1,0:T(2,128)}, s32[2,512]{1,0:T(2,128)S(1)}, u32[]{:S(2)}) copy-start(s32[2,512]{1,0:T(2,128)S(1)} %get-tuple-element.2116) | copy-start | bytes 12292
  102.8 214.3 %copy-start.55 = (s32[1024]{0:T(1024)}, s32[1024]{0:T(1024)S(1)}, u32[]{:S(2)}) copy-start(s32[1024]{0:T(1024)S(1)} %get-tuple-element.2098) | copy-start | bytes 12292
  108.2 85.2 %all-gather.39.cloned.1.call-start = ((), (), s32[]{:S(2)}) async-start(), calls=%async_computation.44 | async-start | bytes 2621440 | tf_op jit(solution)/shard_map/all_gather | solution.py:186
  108.3 199.3 %copy-start.67 = (f32[1,1,1024]{2,1,0:T(1,128)}, f32[1,1,1024]{2,1,0:T(1,128)S(1)}, u32[]{:S(2)}) copy-start(f32[1,1,1024]{2,1,0:T(1,128)S(1)} %get-tuple-element.1160) | copy-start | bytes 12292
  108.3 203.6 %copy-start.69 = (f32[1,1,1024]{2,1,0:T(1,128)}, f32[1,1,1024]{2,1,0:T(1,128)S(1)}, u32[]{:S(2)}) copy-start(f32[1,1,1024]{2,1,0:T(1,128)S(1)} %get-tuple-element.1159) | copy-start | bytes 12292
  108.3 199.2 %copy-start.51 = (f32[1,1,1024]{2,1,0:T(1,128)}, f32[1,1,1024]{2,1,0:T(1,128)S(1)}, u32[]{:S(2)}) copy-start(f32[1,1,1024]{2,1,0:T(1,128)S(1)} %get-tuple-element.1156) | copy-start | bytes 12292
  108.3 199.2 %copy-start.77 = (f32[1,1,1024]{2,1,0:T(1,128)}, f32[1,1,1024]{2,1,0:T(1,128)S(1)}, u32[]{:S(2)}) copy-start(f32[1,1,1024]{2,1,0:T(1,128)S(1)} %get-tuple-element.1157) | copy-start | bytes 12292
  108.3 199.2 %copy-start.88 = (f32[1,1,1024]{2,1,0:T(1,128)}, f32[1,1,1024]{2,1,0:T(1,128)S(1)}, u32[]{:S(2)}) copy-start(f32[1,1,1024]{2,1,0:T(1,128)S(1)} %get-tuple-element.1155) | copy-start | bytes 12292
  108.3 203.6 %copy-start.91 = (f32[1,1,1024]{2,1,0:T(1,128)}, f32[1,1,1024]{2,1,0:T(1,128)S(1)}, u32[]{:S(2)}) copy-start(f32[1,1,1024]{2,1,0:T(1,128)S(1)} %get-tuple-element.1154) | copy-start | bytes 12292
  153.0 154.5 %copy-start.97 = (f32[256]{0:T(256)}, f32[256]{0:T(256)S(1)}, u32[]{:S(2)}) copy-start(f32[256]{0:T(256)S(1)} %broadcast_multiply_fusion.1) | copy-start | bytes 3076
  155.0 152.5 %copy-start.106 = (f32[256]{0:T(256)}, f32[256]{0:T(256)S(1)}, u32[]{:S(2)}) copy-start(f32[256]{0:T(256)S(1)} %fusion.514) | copy-start | bytes 3076
  158.0 72.5 %all-gather.17.cloned.1.call-start = ((), (), s32[]{:S(2)}) async-start(), calls=%async_computation.19 | async-start | bytes 2621440 | tf_op jit(solution)/shard_map/all_gather | solution.py:186
  158.6 110.5 %reduce-scatter.49.cloned.1.call-start = ((), (), s32[]{:S(2)}) async-start(), calls=%async_computation.45 | async-start | bytes 2621440 | tf_op jit(solution)/shard_map/reduce_scatter | solution.py:194
  212.8 94.8 %copy-start.21 = (bf16[2,256,1024]{2,1,0:T(8,128)(2,1)S(1)}, bf16[2,256,1024]{2,1,0:T(8,128)(2,1)}, u32[]{:S(2)}) copy-start(bf16[2,256,1024]{2,1,0:T(8,128)(2,1)} %param.29) | copy-start | bytes 3145732
  212.8 94.7 %reduce-scatter.21.cloned.1.call-start = ((), (), s32[]{:S(2)}) async-start(), calls=%async_computation.20 | async-start | bytes 2621440 | tf_op jit(solution)/shard_map/reduce_scatter | solution.py:194
  246.0 106.5 %all-gather.19.cloned.1.call-start = ((), (), s32[]{:S(2)}) async-start(), calls=%async_computation.21 | async-start | bytes 2621440 | tf_op jit(solution)/shard_map/all_gather | solution.py:144
  312.9 3.3 collective-permute-start
  317.0 104.4 %reduce-scatter.39.cloned.1.call-start = ((), (), s32[]{:S(2)}) async-start(), calls=%async_computation.36 | async-start | bytes 2621440 | tf_op jit(solution)/shard_map/reduce_scatter | solution.py:173
  386.0 73.7 %reduce-scatter.23.cloned.1.call-start = ((), (), s32[]{:S(2)}) async-start(), calls=%async_computation.22 | async-start | bytes 2621440 | tf_op jit(solution)/shard_map/reduce_scatter | solution.py:173
  415.0 86.1 %copy-start.123 = (f32[1,1024]{1,0:T(1,128)S(1)}, f32[1,1024]{1,0:T(1,128)}, u32[]{:S(2)}) copy-start(f32[1,1024]{1,0:T(1,128)} %copy-done.122) | copy-start | bytes 12292
  415.0 86.1 %all-gather.33.cloned.1.call-start = ((), (), s32[]{:S(2)}) async-start(), calls=%async_computation.37 | async-start | bytes 2621440 | tf_op jit(solution)/shard_map/all_gather | solution.py:186
  422.7 192.6 %copy-start.95 = (f32[256]{0:T(256)}, f32[256]{0:T(256)S(1)}, u32[]{:S(2)}) copy-start(f32[256]{0:T(256)S(1)} %broadcast_multiply_fusion.3) | copy-start | bytes 3076
  462.8 152.4 %copy-start.100 = (f32[256]{0:T(256)}, f32[256]{0:T(256)S(1)}, u32[]{:S(2)}) copy-start(f32[256]{0:T(256)S(1)} %fusion.512) | copy-start | bytes 3076
  465.6 72.5 %all-gather.21.cloned.1.call-start = ((), (), s32[]{:S(2)}) async-start(), calls=%async_computation.23 | async-start | bytes 2621440 | tf_op jit(solution)/shard_map/all_gather | solution.py:186
  466.2 110.7 %reduce-scatter.41.cloned.1.call-start = ((), (), s32[]{:S(2)}) async-start(), calls=%async_computation.38 | async-start | bytes 2621440 | tf_op jit(solution)/shard_map/reduce_scatter | solution.py:194
  520.4 94.8 %copy-start.24 = (bf16[256,1024]{1,0:T(8,128)(2,1)S(1)}, bf16[256,1024]{1,0:T(8,128)(2,1)}, u32[]{:S(2)}) copy-start(bf16[256,1024]{1,0:T(8,128)(2,1)} %reduce-scatter.39.cloned.1.call-done) | copy-start | bytes 1572868
  520.5 94.8 %copy-start.89 = (f32[1,1,1024]{2,1,0:T(1,128)S(1)}, f32[1,1,1024]{2,1,0:T(1,128)}, u32[]{:S(2)}) copy-start(f32[1,1,1024]{2,1,0:T(1,128)} %copy-done.88) | copy-start | bytes 12292
  520.5 94.8 %reduce-scatter.25.cloned.1.call-start = ((), (), s32[]{:S(2)}) async-start(), calls=%async_computation.24 | async-start | bytes 2621440 | tf_op jit(solution)/shard_map/reduce_scatter | solution.py:194
  553.7 107.6 %all-gather.23.cloned.1.call-start = ((), (), s32[]{:S(2)}) async-start(), calls=%async_computation.25 | async-start | bytes 2621440 | tf_op jit(solution)/shard_map/all_gather | solution.py:144
  621.7 3.2 collective-permute-start.1
  625.8 105.4 %reduce-scatter.31.cloned.1.call-start = ((), (), s32[]{:S(2)}) async-start(), calls=%async_computation.29 | async-start | bytes 2621440 | tf_op jit(solution)/shard_map/reduce_scatter | solution.py:173
  695.9 75.7 %all-gather.27.cloned.1.call-start = ((), (), s32[]{:S(2)}) async-start(), calls=%async_computation.30 | async-start | bytes 2621440 | tf_op jit(solution)/shard_map/all_gather | solution.py:186
  736.1 90.2 %reduce-scatter.33.cloned.1.call-start = ((), (), s32[]{:S(2)}) async-start(), calls=%async_computation.31 | async-start | bytes 2621440 | tf_op jit(solution)/shard_map/reduce_scatter | solution.py:194
  790.9 76.5 %all-gather.29.cloned.1.call-start = ((), (), s32[]{:S(2)}) async-start(), calls=%async_computation.32 | async-start | bytes 2621440 | tf_op jit(solution)/shard_map/all_gather | solution.py:232
  832.0 81.5 %reduce-scatter.35.cloned.1.call-start = ((), (), s32[]{:S(2)}) async-start(), calls=%async_computation.33 | async-start | bytes 2621440 | tf_op jit(solution)/shard_map/reduce_scatter | solution.py:239
  878.1 73.8 %reduce-scatter.27.cloned.1.call-start = ((), (), s32[]{:S(2)}) async-start(), calls=%async_computation.26 | async-start | bytes 2621440 | tf_op jit(solution)/shard_map/reduce_scatter | solution.py:173
  909.1 85.4 %all-gather.31.cloned.1.call-start = ((), (), s32[]{:S(2)}) async-start(), calls=%async_computation.34 | async-start | bytes 2621440 | tf_op jit(solution)/shard_map/all_gather | solution.py:251
  957.2 151.4 %copy-start.108 = (f32[256]{0:T(256)}, f32[256]{0:T(256)S(1)}, u32[]{:S(2)}) copy-start(f32[256]{0:T(256)S(1)} %negate_multiply_fusion.10) | copy-start | bytes 3076
  959.1 149.5 %reduce-scatter.37.cloned.1.call-start = ((), (), s32[]{:S(2)}) async-start(), calls=%async_computation.35 | async-start | bytes 2621440 | tf_op jit(solution)/shard_map/reduce_scatter | solution.py:288
  1073.3 80.3 %all-gather.35.cloned.1.call-start = ((), (), s32[]{:S(2)}) async-start(), calls=%async_computation.39 | async-start | bytes 2621440 | tf_op jit(solution)/shard_map/all_gather | solution.py:232
  1110.0 3.8 collective-permute-start.2
  1118.1 81.6 %copy-start.17 = (bf16[256,1024]{1,0:T(8,128)(2,1)S(1)}, bf16[256,1024]{1,0:T(8,128)(2,1)}, u32[]{:S(2)}) copy-start(bf16[256,1024]{1,0:T(8,128)(2,1)} %bitcast_select_fusion.3) | copy-start | bytes 1572868
  1118.1 81.6 %copy-start.25 = (bf16[256,1024]{1,0:T(8,128)(2,1)S(1)}, bf16[256,1024]{1,0:T(8,128)(2,1)}, u32[]{:S(2)}) copy-start(bf16[256,1024]{1,0:T(8,128)(2,1)} %reduce-scatter.39.cloned.1.call-done) | copy-start | bytes 1572868
  1118.1 81.5 %copy-start.96 = (f32[256]{0:T(256)S(1)}, f32[256]{0:T(256)}, u32[]{:S(2)}) copy-start(f32[256]{0:T(256)} %copy-done.95) | copy-start | bytes 3076
  1118.1 81.5 %reduce-scatter.43.cloned.1.call-start = ((), (), s32[]{:S(2)}) async-start(), calls=%async_computation.40 | async-start | bytes 2621440 | tf_op jit(solution)/shard_map/reduce_scatter | solution.py:239
  1164.3 76.7 %all-gather.37.cloned.1.call-start = ((), (), s32[]{:S(2)}) async-start(), calls=%async_computation.41 | async-start | bytes 2621440 | tf_op jit(solution)/shard_map/all_gather | solution.py:251
  1203.6 151.7 %copy-start.110 = (f32[256]{0:T(256)}, f32[256]{0:T(256)S(1)}, u32[]{:S(2)}) copy-start(f32[256]{0:T(256)S(1)} %negate_multiply_fusion.8) | copy-start | bytes 3076
  1205.6 149.8 %reduce-scatter.45.cloned.1.call-start = ((), (), s32[]{:S(2)}) async-start(), calls=%async_computation.42 | async-start | bytes 2621440 | tf_op jit(solution)/shard_map/reduce_scatter | solution.py:288
  1320.0 80.3 %all-gather.41.cloned.1.call-start = ((), (), s32[]{:S(2)}) async-start(), calls=%async_computation.46 | async-start | bytes 2621440 | tf_op jit(solution)/shard_map/all_gather | solution.py:232
  1356.7 3.8 collective-permute-start.3
  1364.9 81.6 %copy-start.15 = (bf16[256,1024]{1,0:T(8,128)(2,1)S(1)}, bf16[256,1024]{1,0:T(8,128)(2,1)}, u32[]{:S(2)}) copy-start(bf16[256,1024]{1,0:T(8,128)(2,1)} %bitcast_select_fusion.2) | copy-start | bytes 1572868
  1364.9 81.5 %copy-start.26 = (bf16[256,1024]{1,0:T(8,128)(2,1)S(1)}, bf16[256,1024]{1,0:T(8,128)(2,1)}, u32[]{:S(2)}) copy-start(bf16[256,1024]{1,0:T(8,128)(2,1)} %reduce-scatter.47.cloned.1.call-done) | copy-start | bytes 1572868
  1364.9 81.5 %reduce-scatter.51.cloned.1.call-start = ((), (), s32[]{:S(2)}) async-start(), calls=%async_computation.47 | async-start | bytes 2621440 | tf_op jit(solution)/shard_map/reduce_scatter | solution.py:239
  1411.1 75.4 %all-gather.25.cloned.1.call-start = ((), (), s32[]{:S(2)}) async-start(), calls=%async_computation.27 | async-start | bytes 2621440 | tf_op jit(solution)/shard_map/all_gather | solution.py:186
  1451.0 86.5 %copy-start.90 = (f32[1,1,1024]{2,1,0:T(1,128)S(1)}, f32[1,1,1024]{2,1,0:T(1,128)}, u32[]{:S(2)}) copy-start(f32[1,1,1024]{2,1,0:T(1,128)} %copy-done.88) | copy-start | bytes 12292
  1451.1 86.5 %copy-start.107 = (f32[256]{0:T(256)S(1)}, f32[256]{0:T(256)}, u32[]{:S(2)}) copy-start(f32[256]{0:T(256)} %copy-done.106) | copy-start | bytes 3076
  1451.1 86.5 %reduce-scatter.29.cloned.1.call-start = ((), (), s32[]{:S(2)}) async-start(), calls=%async_computation.28 | async-start | bytes 2621440 | tf_op jit(solution)/shard_map/reduce_scatter | solution.py:194
  1502.2 76.6 %all-gather.43.cloned.1.call-start = ((), (), s32[]{:S(2)}) async-start(), calls=%async_computation.48 | async-start | bytes 2621440 | tf_op jit(solution)/shard_map/all_gather | solution.py:251
  1543.3 145.3 %all-reduce.11.cloned.1.call-start = ((), (), s32[]{:S(2)}) async-start(), calls=%async_computation.50 | async-start | bytes 131072 | tf_op jit(solution)/shard_map/psum | solution.py:363
  1654.5 72.6 %reduce-scatter.53.cloned.1.call-start = ((), (), s32[]{:S(2)}) async-start(), calls=%async_computation.49 | async-start | bytes 2621440 | tf_op jit(solution)/shard_map/reduce_scatter | solution.py:288
  (128 other events, 2469.8 us)
Sparse Core Ops, SparseCore 0:
  10.5 38.0 all-gather.44
  77.5 35.1 reduce-scatter.46
  116.0 35.1 reduce-scatter.18
  158.1 35.2 all-gather.38
  195.1 35.2 all-gather.16
  233.8 35.1 reduce-scatter.48
  272.3 35.1 reduce-scatter.20
  317.1 35.3 all-gather.18
  386.1 35.1 reduce-scatter.38
  424.4 35.1 reduce-scatter.22
  465.8 35.2 all-gather.32
  502.8 35.2 all-gather.20
  541.7 35.1 reduce-scatter.40
  580.0 35.1 reduce-scatter.24
  625.9 35.3 all-gather.22
  696.0 35.1 reduce-scatter.30
  736.2 35.2 all-gather.26
  791.0 35.1 reduce-scatter.32
  832.1 35.2 all-gather.28
  878.3 35.1 reduce-scatter.34
  916.7 35.1 reduce-scatter.26
  959.2 35.2 all-gather.30
  1073.4 35.1 reduce-scatter.36
  1118.2 35.2 all-gather.34
  1164.4 35.1 reduce-scatter.42
  1205.7 35.2 all-gather.36
  1320.1 35.1 reduce-scatter.44
  1365.0 35.2 all-gather.40
  1411.2 35.1 reduce-scatter.50
  1451.2 35.2 all-gather.24
  1502.3 35.1 reduce-scatter.28
  1543.5 35.2 all-gather.42
  1654.6 33.9 all-reduce.10
  1692.2 34.8 reduce-scatter.52
where the time goes:
time: 1750 us; the launch traced here: 1740 us
  waiting for transfers between devices  1050 us (60%)
  matrix products  392 us (22%)
  other arithmetic  169 us (10%)
  local copies, waits for them, and re-layouts  96.4 us (6%)
    reduce_scatter x6, waiting for transfers between devices, forward_split(): lax.psum_scatter(jnp.dot(active_units, down_matrix, preferred_element_typ...  193 us
    all_gather x6, waiting for transfers between devices, forward_split(): lax.all_gather(middle.astype(jnp.bfloat16), 'tensor', axis=0, tiled=True)  175 us
    reduce_scatter x6, waiting for transfers between devices, forward_split(): lax.psum_scatter(jnp.dot(merged_heads, output_matrix, preferred_element_t...  160 us
    reduce_scatter x3, waiting for transfers between devices, backward_split(): lax.psum_scatter(along_rows(grad_projected, query_key_value_matrix).astyp...  108 us
    all_gather x3, waiting for transfers between devices, backward_split(): lax.all_gather(grad_second.astype(jnp.bfloat16), 'tensor', axis=0, tiled=...  106 us
    all_gather x3, waiting for transfers between devices, forward_split(): lax.all_gather(inputs.astype(jnp.bfloat16), 'tensor', axis=0, tiled=True)  106 us
    all_gather x3, waiting for transfers between devices, backward_split(): lax.all_gather(grad_first.astype(jnp.bfloat16), 'tensor', axis=0, tiled=T...  102 us
    reduce_scatter x3, waiting for transfers between devices, backward_split(): lax.psum_scatter(along_rows(grad_hidden, up_matrix).astype(jnp.bfloat16),...  74.9 us
  transfers between devices with their start and end apart: 38, of which 38 were waited for; matrix products, arithmetic and copies ran while one was open for 10% of the time, Pallas kernels for 0%

commit v1 on v0

v1 whole, which is shorter than its diff:
```python
import functools

import jax
import jax.numpy as jnp
from jax import lax
from jax.experimental import pallas as pl
from jax.experimental.pallas import tpu as pltpu
from jax.sharding import PartitionSpec as P

D = 1024
HEAD = 64
PAIR = 2 * HEAD
PREFIX = 64
LEN = 1024
SPAN = LEN // 32
LABELS = 128
HIDDEN = -1e30
F32 = jnp.float32
BF16 = jnp.bfloat16


def dot(a, b):
    return jnp.dot(a, b, preferred_element_type=F32)


def dot_t(a, b):
    return lax.dot_general(a, b, (((1,), (1,)), ((), ())), preferred_element_type=F32)


def head_lanes(rows, head):
    lanes = lax.broadcasted_iota(jnp.int32, (rows, PAIR), 1)
    return (lanes >= head * HEAD) & (lanes < (head + 1) * HEAD)


def fill_keys(keys, own, sib, pre, own_lab, sib_lab):
    rows = own.shape[0]
    keys[:rows, :PAIR] = own[...]
    keys[rows : 2 * rows, :PAIR] = sib[...]
    keys[2 * rows :, :PAIR] = pre[...]
    keys[:rows, PAIR:] = own_lab[...]
    keys[rows : 2 * rows, PAIR:] = sib_lab[...]
    keys[2 * rows :, PAIR:] = jnp.zeros((PREFIX, LABELS), BF16)


def attend_kernel(block, q, ko, vo, ks, vs, kp, vp, lab_q, lab_o, lab_s, out, lse, keys, vals_t):
    rows = q.shape[0]
    fill_keys(keys, ko, ks, kp, lab_o, lab_s)
    vals_t[:, :rows] = vo[...].T
    vals_t[:, rows : 2 * rows] = vs[...].T
    vals_t[:, 2 * rows :] = vp[...].T
    for start in range(0, rows, block):
        part = pl.ds(start, block)
        query = q[part, :] * 0.125
        label = lab_q[part, :]
        results = []
        for head in range(2):
            mine = jnp.where(head_lanes(block, head), query, 0)
            scores = dot_t(keys[...], jnp.concatenate([mine, label], 1))
            peak = jnp.max(scores, axis=0, keepdims=True)
            weights = jnp.exp(scores - peak)
            total = jnp.sum(weights, axis=0, keepdims=True)
            merged = dot(vals_t[head * HEAD : (head + 1) * HEAD, :], weights.astype(BF16))
            results.append(merged / total)
            lse[0, head : head + 1, part] = peak + jnp.log(total)
        out[part, :] = jnp.concatenate(results, 0).T.astype(BF16)


def attend_back_kernel(
    block, q, ko, vo, ks, vs, kp, vp, lab_q, lab_o, lab_s, out, lse, grad,
    dq, dko, dvo, dks, dvs, dkp, dvp, keys, vals, keys_t, dk_sum, dv_sum,
):
    rows = q.shape[0]
    fill_keys(keys, ko, ks, kp, lab_o, lab_s)
    vals[:rows, :] = vo[...]
    vals[rows : 2 * rows, :] = vs[...]
    vals[2 * rows :, :] = vp[...]
    keys_t[:, :rows] = ko[...].T
    keys_t[:, rows : 2 * rows] = ks[...].T
    keys_t[:, 2 * rows :] = kp[...].T
    for start in range(0, rows, block):
        part = pl.ds(start, block)
        query = q[part, :] * 0.125
        label = lab_q[part, :]
        grad_part = grad[part, :]
        product = (grad_part.astype(F32) * out[part, :].astype(F32)).T
        queries, grads, weights_all, scores_all, results = [], [], [], [], []
        for head in range(2):
            span = slice(head * HEAD, (head + 1) * HEAD)
            mine = jnp.where(head_lanes(block, head), query, 0)
            mine_grad = jnp.where(head_lanes(block, head), grad_part, 0)
            scores = dot_t(keys[...], jnp.concatenate([mine, label], 1))
            weights = jnp.exp(scores - lse[0, head : head + 1, part])
            delta = jnp.sum(product[span], axis=0, keepdims=True)
            grad_scores = (weights * (dot_t(vals[...], mine_grad) - delta)).astype(BF16)
            results.append(dot(keys_t[span, :], grad_scores))
            queries.append(mine)
            grads.append(mine_grad)
            weights_all.append(weights.astype(BF16))
            scores_all.append(grad_scores)
        dq[part, :] = (jnp.concatenate(results, 0).T * 0.125).astype(BF16)
        dv_part = dot(jnp.concatenate(weights_all, 1), jnp.concatenate(grads, 0))
        dk_part = dot(jnp.concatenate(scores_all, 1), jnp.concatenate(queries, 0))
        if start == 0:
            dv_sum[...] = dv_part
            dk_sum[...] = dk_part
        else:
            dv_sum[...] += dv_part
            dk_sum[...] += dk_part
    dko[...] = dk_sum[:rows, :]
    dvo[...] = dv_sum[:rows, :]
    dks[...] = dk_sum[rows : 2 * rows, :].astype(BF16)
    dvs[...] = dv_sum[rows : 2 * rows, :].astype(BF16)
    dkp[...] = dk_sum[2 * rows :, :]
    dvp[...] = dv_sum[2 * rows :, :]


def attention_specs(rows, pairs):
    def column(height, offset):
        return pl.BlockSpec((height, PAIR), lambda p: (0, offset + p))

    labels = pl.BlockSpec((rows, LABELS), lambda p: (0, 0))
    ins = [
        column(rows, 0), column(rows, pairs), column(rows, 2 * pairs),
        column(rows, 0), column(rows, pairs),
        column(PREFIX, 0), column(PREFIX, 0),
        labels, labels, labels,
    ]
    return column, ins, pl.BlockSpec((1, 8, rows), lambda p: (p, 0, 0))


def attend(qkv, kv_sib, pre, labels):
    rows, width = qkv.shape[0], qkv.shape[1] // 3
    pairs = width // PAIR
    column, ins, lse_spec = attention_specs(rows, pairs)
    size = 2 * rows + PREFIX
    return pl.pallas_call(
        functools.partial(attend_kernel, min(rows, 256)),
        grid=(pairs,),
        in_specs=ins,
        out_specs=[column(rows, 0), lse_spec],
        out_shape=[
            jax.ShapeDtypeStruct((rows, width), BF16),
            jax.ShapeDtypeStruct((pairs, 8, rows), F32),
        ],
        scratch_shapes=[pltpu.VMEM((size, PAIR + LABELS), BF16), pltpu.VMEM((PAIR, size), BF16)],
        compiler_params=pltpu.CompilerParams(vmem_limit_bytes=40 << 20),
        cost_estimate=pl.CostEstimate(
            flops=2 * 2 * rows * size * width, transcendentals=rows * size * width // HEAD,
            bytes_accessed=16 * rows * width,
        ),
        name="attend",
    )(qkv, qkv, qkv, kv_sib, kv_sib, pre[0], pre[1], *labels)


def attend_back(qkv, kv_sib, pre, labels, merged, lse, grad):
    rows, width = qkv.shape[0], qkv.shape[1] // 3
    pairs = width // PAIR
    column, ins, lse_spec = attention_specs(rows, pairs)
    size = 2 * rows + PREFIX
    shape = jax.ShapeDtypeStruct
    return pl.pallas_call(
        functools.partial(attend_back_kernel, min(rows, 256)),
        grid=(pairs,),
        in_specs=ins + [column(rows, 0), lse_spec, column(rows, 0)],
        out_specs=[column(rows, 0)] * 5 + [column(PREFIX, 0)] * 2,
        out_shape=[
            shape((rows, width), BF16),
            shape((rows, width), F32), shape((rows, width), F32),
            shape((rows, width), BF16), shape((rows, width), BF16),
            shape((PREFIX, width), F32), shape((PREFIX, width), F32),
        ],
        scratch_shapes=[
            pltpu.VMEM((size, PAIR + LABELS), BF16), pltpu.VMEM((size, PAIR), BF16),
            pltpu.VMEM((PAIR, size), BF16), pltpu.VMEM((size, PAIR), F32), pltpu.VMEM((size, PAIR), F32),
        ],
        compiler_params=pltpu.CompilerParams(vmem_limit_bytes=40 << 20),
        cost_estimate=pl.CostEstimate(
            flops=5 * 2 * rows * size * width, transcendentals=rows * size * width // HEAD,
            bytes_accessed=32 * rows * width,
        ),
        name="attend_back",
    )(qkv, qkv, qkv, kv_sib, kv_sib, pre[0], pre[1], *labels, merged, lse, grad)


def norm_stats(values):
    center = values - jnp.mean(values, axis=-1, keepdims=True)
    scale = lax.rsqrt(jnp.mean(center * center, axis=-1, keepdims=True) + 1e-05)
    return center * scale, scale


def norm_back(grad, gain, normed, scale):
    dn = grad * gain
    return scale * (
        dn
        - jnp.mean(dn, axis=-1, keepdims=True)
        - normed * jnp.mean(dn * normed, axis=-1, keepdims=True)
    )


def gelu_pair(u):
    cdf = 0.5 * (1.0 + lax.erf(u * 0.7071067811865476))
    pdf = jnp.exp(-0.5 * u * u) * 0.3989422804014327
    return (u * cdf).astype(BF16), (cdf + u * pdf).astype(BF16)


class Links:
    def __init__(self):
        self.core = lax.axis_index("section")
        self.place = lax.axis_index("tensor")
        self.size = lax.axis_size("tensor")
        self.low = self.place % 2
        self.high = self.place // 2
        self.group = self.size // 2

    def sibling(self, a, only=None):
        pairs = [(0, 1), (1, 0)] if only is None else [(only, 1 - only)]
        return lax.ppermute(a, "section", pairs)

    def across(self, a, only=None):
        if only is None:
            return lax.ppermute(a, "tensor", [(t, t ^ 1) for t in range(self.size)])
        pairs = [(only * self.size + t, only * self.size + (t ^ 1)) for t in range(self.size)]
        return lax.ppermute(a, ("section", "tensor"), pairs)

    def diagonal(self, a, source):
        pairs = [(source * self.size + t, (1 - source) * self.size + (t ^ 1)) for t in range(self.size)]
        return lax.ppermute(a, ("section", "tensor"), pairs)

    def from_ahead(self, a, by):
        g = self.group
        pairs = [(2 * ((h + by) % g) + p, 2 * h + p) for h in range(g) for p in range(2)]
        return lax.ppermute(a, "tensor", pairs)

    def gather(self, a):
        return [a] + [self.from_ahead(a, k) for k in range(1, self.group)]

    def scatter_sum(self, part_fn):
        arrived = [self.from_ahead(part_fn(k).astype(BF16), self.group - k) for k in range(1, self.group)]
        total = part_fn(0)
        for a in arrived:
            total = total + a.astype(F32)
        return total


def forward(links, x, weights, pre, labels):
    qkv_w, out_w, up_w, up_b, down_w, gains, shifts = weights
    width = out_w.shape[0]
    blocks = [dot(b, qkv_w).astype(BF16) for b in links.gather(x)]
    qkv = jnp.concatenate(blocks, 0)
    kv_sib = links.sibling(qkv[:, width:])
    merged, lse = attend(qkv, kv_sib, pre, labels)
    rows = x.shape[0]
    attended = links.scatter_sum(lambda k: dot(merged[k * rows : (k + 1) * rows], out_w)) + shifts[0]
    normed_first, scale_first = norm_stats(x.astype(F32) + attended)
    middle = normed_first * gains[0] + shifts[1]
    blocks = links.gather(middle.astype(BF16))
    pairs = [gelu_pair(dot(b, up_w) + up_b) for b in blocks]
    branch = links.scatter_sum(lambda k: dot(pairs[k][0], down_w)) + shifts[2]
    normed_last, scale_last = norm_stats(middle + branch)
    result = (normed_last * gains[1] + shifts[3]).astype(BF16)
    slopes = [p[1] for p in pairs]
    return result, (qkv, kv_sib, merged, lse, normed_first, scale_first, slopes, normed_last, scale_last)


def backward(links, grad, weights, pre, labels, kept):
    qkv_w, out_w, up_w, up_b, down_w, gains, shifts = weights
    qkv, kv_sib, merged, lse, normed_first, scale_first, slopes, normed_last, scale_last = kept
    rows = grad.shape[0]
    grad_second = norm_back(grad.astype(F32), gains[1], normed_last, scale_last)
    blocks = links.gather(grad_second.astype(BF16))
    hiddens = [
        (dot_t(b, down_w) * s.astype(F32)).astype(BF16) for b, s in zip(blocks, slopes, strict=True)
    ]
    grad_middle = grad_second + links.scatter_sum(lambda k: dot_t(hiddens[k], up_w))
    grad_first = norm_back(grad_middle, gains[0], normed_first, scale_first)
    blocks = links.gather(grad_first.astype(BF16))
    grad_merged = jnp.concatenate([dot_t(b, out_w).astype(BF16) for b in blocks], 0)
    dq, dko, dvo, dks, dvs, dkp, dvp = attend_back(qkv, kv_sib, pre, labels, merged, lse, grad_merged)
    arrived = links.sibling(jnp.concatenate([dks, dvs], 1)).astype(F32)
    width = out_w.shape[0]
    dk = (dko + arrived[:, :width]).astype(BF16)
    dv = (dvo + arrived[:, width:]).astype(BF16)
    dqkv = jnp.concatenate([dq, dk, dv], 1)
    grad_inputs = grad_first + links.scatter_sum(
        lambda k: dot_t(dqkv[k * rows : (k + 1) * rows], qkv_w)
    )
    return grad_inputs, jnp.stack([dkp, dvp])


def spread_weights(links, arrays):
    first = links.core == 0
    layers = ([], [])
    for layer in range(2):
        for a in arrays:
            other = links.across(a, layer)
            sib_a, sib_other = links.sibling(a, layer), links.sibling(other, layer)
            here = links.core == layer
            layers[layer].append((jnp.where(here, a, sib_a), jnp.where(here, other, sib_other)))
    return layers


def sum_over_dp(a):
    size = lax.axis_size("dp")
    step = 1
    if size & (size - 1):
        return lax.psum(a, "dp")
    while step < size:
        a = a + lax.ppermute(a, "dp", [(i, i ^ step) for i in range(size)])
        step *= 2
    return a


def local(
    states, segment_ids, cotangent, qkv_weight, out_weight, up_weight, up_bias, down_weight,
    norm_gain, shift_vec, prefix,
):
    links = Links()
    first = links.core == 0
    low = links.low

    def arrange(both):
        mine = lax.dynamic_index_in_dim(both, low, 0, keepdims=False)
        other = lax.dynamic_index_in_dim(both, 1 - low, 0, keepdims=False)
        return jnp.where(first, mine, links.across(other, 1))

    x = arrange(states)
    grad = arrange(cotangent)

    segment = lax.dynamic_index_in_dim(segment_ids, low, 0, keepdims=False)
    classes = (segment[-1] - segment).reshape(links.group, 2, -1)
    classes = jnp.roll(classes, -links.high, 0)
    parity = jnp.where(first, low, 1 - low)
    own = lax.dynamic_index_in_dim(classes, parity, 1, keepdims=False).reshape(-1)
    sib = lax.dynamic_index_in_dim(classes, 1 - parity, 1, keepdims=False).reshape(-1)
    numbers = jnp.arange(LABELS)[None, :]
    label_q = (own[:, None] == numbers).astype(BF16)
    known = numbers <= 2 * SPAN
    label_o = jnp.where(known & (own[:, None] != numbers), HIDDEN, 0.0).astype(BF16)
    label_s = jnp.where(known & (sib[:, None] != numbers), HIDDEN, 0.0).astype(BF16)
    labels = (label_q, label_o, label_s)

    small = jnp.concatenate(
        [norm_gain[0], shift_vec[0]], 0
    )
    small_sib = links.sibling(small)
    layers = spread_weights(
        links,
        [jnp.transpose(qkv_weight[0], (1, 0, 2)), prefix[0], out_weight[0], up_weight[0], up_bias, down_weight[0]],
    )
    weights, prefixes = [], []
    for layer in range(2):
        qkv, pre, out, up, bias, down = layers[layer]
        vectors = jnp.where(links.core == layer, small, small_sib).astype(F32)
        weights.append((
            jnp.concatenate([p[i] for i in range(3) for p in qkv], 1),
            jnp.concatenate(out, 0),
            jnp.concatenate(up, 1),
            jnp.concatenate(bias, 1).astype(F32),
            jnp.concatenate(down, 0),
            vectors[:2],
            vectors[2:],
        ))
        prefixes.append(jnp.concatenate(pre, 2))

    y0, kept0 = forward(links, x, weights[0], prefixes[0], labels)
    y1, kept1 = forward(links, y0, weights[1], prefixes[1], labels)
    g1, p1 = backward(links, grad, weights[1], prefixes[1], labels, kept1)
    g0, p0 = backward(links, g1.astype(BF16), weights[0], prefixes[0], labels, kept0)

    def deliver(first_layer, second_layer, wire, dtype):
        near = jnp.where(first, first_layer.astype(dtype), links.sibling(second_layer.astype(wire), 0).astype(dtype))
        far0 = links.diagonal(first_layer.astype(wire), 1)
        far1 = links.across(second_layer.astype(wire), 1)
        far = jnp.where(first, far0, far1).astype(dtype)
        return jnp.stack([jnp.where(low == 0, near, far), jnp.where(low == 0, far, near)])

    hidden_out = deliver(y0, y1, BF16, BF16)
    input_grads = deliver(g0, g1, BF16, F32)

    total = jnp.where(first, p0, p1) + links.sibling(jnp.where(first, p1, p0))
    quarter = total.shape[-1] // 2
    total = total[..., :quarter] + links.across(total[..., quarter:])
    prefix_grads = sum_over_dp(total)
    return hidden_out[None], input_grads[None], prefix_grads[None]


def solution(mesh):
    placed = (
        P(None, ("dp", "tensor"), None),
        P(None, "dp"),
        P(None, ("dp", "tensor"), None),
        P("section", None, None, "tensor"),
        P("section", "tensor", None),
        P("section", None, "tensor"),
        P("section", "tensor"),
        P("section", "tensor", None),
        P("section", None, None),
        P("section", None, None),
        P("section", None, None, "tensor"),
    )
    return jax.shard_map(
        local,
        mesh=mesh,
        in_specs=placed,
        out_specs=(
            P("section", None, ("dp", "tensor"), None),
            P("section", None, ("dp", "tensor"), None),
            P("section", None, None, "tensor"),
        ),
        check_vma=False,
    )
```

time: 1750 us -> 499 us (0.29)
  waiting for transfers between devices: 1050 us -> 229 us
  matrix products: 392 us -> 59.8 us
  other arithmetic: 169 us -> 33.4 us
  starting transfers between devices: 10.2 us -> 96 us
  local copies, waits for them, and re-layouts: 96.4 us -> 13 us
  Pallas kernels: 0 us -> 54.3 us
    reduce_scatter x18 -> x0, waiting for transfers between devices: 535 us -> none  [the longest x6 193 us: forward_split(): lax.psum_scatter(jnp.dot(active_units, down_matrix, preferred_element_typ...]
    all_gather x15 -> x0, waiting for transfers between devices: 489 us -> none  [the longest x6 175 us: forward_split(): lax.all_gather(middle.astype(jnp.bfloat16), 'tensor', axis=0, tiled=True)]
    dot_general x75 -> x28, matrix products: 365 us -> 59.8 us  [the longest x12 43.3 us: dot_t(): lax.dot_general(a, b, (((1,), (1,)), ((), ())), preferred_element_type=F32)]
    ppermute x4 -> x69, waiting for transfers between devices: 7.94 us -> 229 us  [the longest x16 162 us: from_ahead(): return lax.ppermute(a, 'tensor', pairs)]
    ppermute x4 -> x69, starting transfers between devices: 6.09 us -> 96 us  [the longest x32 53.1 us: sibling(): return lax.ppermute(a, 'section', pairs)]
    convert_element_type x19 -> x16, other arithmetic: 82.1 us -> 9.4 us  [the longest x2 3.82 us: backward(): blocks = links.gather(grad_first.astype(BF16))]
    reduce_sum x31 -> x5, other arithmetic: 56 us -> 1.44 us  [the longest x4 0.99 us: norm_stats(): scale = lax.rsqrt(jnp.mean(center * center, axis=-1, keepdims=True) + 1e-05)]
    pallas_call x0 -> x4, Pallas kernels: none -> 54.3 us  [the longest x2 29.1 us: attend_back(): pl.pallas_call(functools.partial(attend_back_kernel, min(rows, 256)), gri...]
  transfers between devices with their start and end apart: 38 -> 69, of which waited for: 38 -> 29; matrix products, arithmetic and copies ran while one was open for 10% -> 10% of each run, Pallas kernels for 0% -> 5%
where the time goes in v1:
time: 499 us; the launch traced here: 489 us
  waiting for transfers between devices  229 us (46%)
  starting transfers between devices  96 us (19%)
  matrix products  59.8 us (12%)
  Pallas kernels  54.3 us (11%)
  other arithmetic  33.4 us (7%)
  local copies, waits for them, and re-layouts  13 us (3%)
    ppermute x16, waiting for transfers between devices, from_ahead(): return lax.ppermute(a, 'tensor', pairs)  162 us
    ppermute x32, starting transfers between devices, sibling(): return lax.ppermute(a, 'section', pairs)  53.1 us
    dot_general x12, matrix products, dot_t(): lax.dot_general(a, b, (((1,), (1,)), ((), ())), preferred_element_type=F32)  43.3 us
    ppermute x16, waiting for transfers between devices, across(): return lax.ppermute(a, ('section', 'tensor'), pairs)  41.3 us
    pallas_call x2, Pallas kernels, attend_back(): pl.pallas_call(functools.partial(attend_back_kernel, min(rows, 256)), gri...  29.1 us
    ppermute x16, starting transfers between devices, across(): return lax.ppermute(a, ('section', 'tensor'), pairs)  26.9 us
    pallas_call x2, Pallas kernels, attend(): pl.pallas_call(functools.partial(attend_kernel, min(rows, 256)), grid=(pa...  25.3 us
    ppermute x32, waiting for transfers between devices, sibling(): return lax.ppermute(a, 'section', pairs)  18.7 us
  transfers between devices with their start and end apart: 69, of which 29 were waited for; matrix products, arithmetic and copies ran while one was open for 10% of the time, Pallas kernels for 5%

profile of v1, /device:TPU:0, one launch (start us, length us, event | category | flops | bytes accessed | tf_op | source)
XLA Modules:
  0.0 489.1 jit_solution(10267233219106771972)
XLA Ops:
  0.6 4.8 collective-permute-start.18
  6.8 4.2 collective-permute-start.17
  11.0 1.9 collective-permute-start.2
  16.8 1.9 dynamic-slice_bitcast_fusion.1
  18.7 1.9 collective-permute-start.19
  22.8 3.2 collective-permute-start.1
  32.1 3.9 collective-permute-start.7
  36.6 13.0 %collective-permute-done.7 = bf16[2,64,256]{2,1,0:T(8,128)(2,1)S(1)} collective-permute-done((bf16[2,64,256]{2,1,0:T(8,128)(2,1)}, bf16[2,64,256]{2,1,0:T(8,128)(2,1)S(1)}, u32[]{:S(2)}, u32[]{:S(2)}) %collective-permute-start.7) | collective-permute-done | bytes 65568 | tf_op jit(solution)/shard_map/ppermute | solution.py:223
  52.0 2.2 collective-permute-start.8
  55.9 3.6 collective-permute-start.3
  64.8 3.6 collective-permute-start.10
  68.4 2.3 collective-permute-start.9
  74.1 3.3 collective-permute-start.14
  77.9 1.6 collective-permute-start.4
  80.9 2.7 collective-permute-start.15
  84.6 6.4 %collective-permute-done.4 = bf16[256,1024]{1,0:T(8,128)(2,1)S(1)} collective-permute-done((bf16[256,1024]{1,0:T(8,128)(2,1)S(1)}, bf16[256,1024]{1,0:T(8,128)(2,1)S(1)}, u32[]{:S(2)}, u32[]{:S(2)}) %collective-permute-start.4) | collective-permute-done | bytes 524320 | tf_op jit(solution)/shard_map/ppermute | solution.py:232
  92.3 2.2 collective-permute-start.21
  94.6 3.0 collective-permute-start.20
  98.8 1.9 broadcast_select_fusion.13
  100.8 2.4 broadcast_select_fusion.3
  103.3 6.2 %collective-permute-done.15 = bf16[1024,1024]{1,0:T(8,128)(2,1)S(1)} collective-permute-done((bf16[1024,1024]{1,0:T(8,128)(2,1)S(1)}, bf16[1024,1024]{1,0:T(8,128)(2,1)S(1)}, u32[]{:S(2)}, u32[]{:S(2)}) %collective-permute-start.15) | collective-permute-done | bytes 2097184 | tf_op jit(solution)/shard_map/ppermute | solution.py:223
  111.7 12.6 %attend.2 = (bf16[512,512]{1,0:T(8,128)(2,1)S(1)}, f32[4,8,512]{2,1,0:T(8,128)S(1)}) custom-call(bf16[512,1536]{1,0:T(8,128)(2,1)S(1)} %pad_maximum_fusion.4.q.ko.vo, bf16[512,1536]{1,0:T(8,128)(2,1)S(1)} %pad_maximum_fusion.4.q.ko.vo, bf16[512,1536]{1,0:T(8,128)(2,1)S(1)} %pad_maximum_fusion.4.q.ko.vo, bf16[512,1024]{1,0:T(8,128)(2,1)S(1)} %collective-permute-done.5.ks.vs, ...), custom_call_target="tpu_custom_call" | custom-call | flops 1140850688 | bytes 4194304 | tf_op jit(solution)/shard_map/attend/pallas_call | solution.py:136
  126.2 22.0 %collective-permute-done.21 = bf16[1024,1024]{1,0:T(8,128)(2,1)S(1)} collective-permute-done((bf16[1024,1024]{1,0:T(8,128)(2,1)S(1)}, bf16[1024,1024]{1,0:T(8,128)(2,1)S(1)}, u32[]{:S(2)}, u32[]{:S(2)}) %collective-permute-start.21) | collective-permute-done | bytes 2097184 | tf_op jit(solution)/shard_map/ppermute | solution.py:223
  149.7 3.3 broadcast_select_fusion.1
  154.7 4.2 collective-permute-done.12
  162.0 14.1 %collective-permute-done.23 = bf16[256,1024]{1,0:T(8,128)(2,1)S(1)} collective-permute-done((bf16[256,1024]{1,0:T(8,128)(2,1)S(1)}, bf16[256,1024]{1,0:T(8,128)(2,1)S(1)}, u32[]{:S(2)}, u32[]{:S(2)}) %collective-permute-start.23) | collective-permute-done | bytes 524320 | tf_op jit(solution)/shard_map/ppermute | solution.py:232
  181.3 11.3 %collective-permute-done.24 = bf16[256,1024]{1,0:T(8,128)(2,1)S(1)} collective-permute-done((bf16[256,1024]{1,0:T(8,128)(2,1)S(1)}, bf16[256,1024]{1,0:T(8,128)(2,1)S(1)}, u32[]{:S(2)}, u32[]{:S(2)}) %collective-permute-start.24) | collective-permute-done | bytes 524320 | tf_op jit(solution)/shard_map/ppermute | solution.py:232
  192.7 1.5 fusion.105
  196.2 11.8 %collective-permute-done.28 = bf16[256,1024]{1,0:T(8,128)(2,1)S(1)} collective-permute-done((bf16[256,1024]{1,0:T(8,128)(2,1)S(1)}, bf16[256,1024]{1,0:T(8,128)(2,1)S(1)}, u32[]{:S(2)}, u32[]{:S(2)}) %collective-permute-start.28) | collective-permute-done | bytes 524320 | tf_op jit(solution)/shard_map/ppermute | solution.py:232
  211.7 5.0 %collective-permute-done.32 = bf16[2,64,256]{2,1,0:T(8,128)(2,1)S(1)} collective-permute-done((bf16[2,64,256]{2,1,0:T(8,128)(2,1)S(1)}, bf16[2,64,256]{2,1,0:T(8,128)(2,1)S(1)}, u32[]{:S(2)}, u32[]{:S(2)}) %collective-permute-start.32) | collective-permute-done | bytes 65568 | tf_op jit(solution)/shard_map/ppermute | solution.py:217
  218.2 1.7 collective-permute-start.45
  220.0 12.6 %attend.3 = (bf16[512,512]{1,0:T(8,128)(2,1)S(1)}, f32[4,8,512]{2,1,0:T(8,128)S(1)}) custom-call(bf16[512,1536]{1,0:T(8,128)(2,1)S(1)} %pad_maximum_fusion.5.q.ko.vo, bf16[512,1536]{1,0:T(8,128)(2,1)S(1)} %pad_maximum_fusion.5.q.ko.vo, bf16[512,1536]{1,0:T(8,128)(2,1)S(1)} %pad_maximum_fusion.5.q.ko.vo, bf16[512,1024]{1,0:T(8,128)(2,1)S(1)} %collective-permute-done.29.ks.vs, ...), custom_call_target="tpu_custom_call" | custom-call | flops 1140850688 | bytes 4194304 | tf_op jit(solution)/shard_map/attend/pallas_call | solution.py:136
  235.9 5.7 %collective-permute-done.42 = bf16[1,1024]{1,0:T(2,128)(2,1)S(1)} collective-permute-done((bf16[1,1024]{1,0:T(2,128)(2,1)S(1)}, bf16[1,1024]{1,0:T(2,128)(2,1)S(1)}, u32[]{:S(2)}, u32[]{:S(2)}) %collective-permute-start.42) | collective-permute-done | bytes 2080 | tf_op jit(solution)/shard_map/ppermute | solution.py:217
  241.6 6.1 %collective-permute-done.36 = bf16[256,1024]{1,0:T(8,128)(2,1)S(1)} collective-permute-done((bf16[256,1024]{1,0:T(8,128)(2,1)S(1)}, bf16[256,1024]{1,0:T(8,128)(2,1)S(1)}, u32[]{:S(2)}, u32[]{:S(2)}) %collective-permute-start.36) | collective-permute-done | bytes 524320 | tf_op jit(solution)/shard_map/ppermute | solution.py:232
  250.1 12.9 %collective-permute-done.46 = bf16[256,1024]{1,0:T(8,128)(2,1)S(1)} collective-permute-done((bf16[256,1024]{1,0:T(8,128)(2,1)S(1)}, bf16[256,1024]{1,0:T(8,128)(2,1)S(1)}, u32[]{:S(2)}, u32[]{:S(2)}) %collective-permute-start.46) | collective-permute-done | bytes 524320 | tf_op jit(solution)/shard_map/ppermute | solution.py:232
  268.7 10.3 %collective-permute-done.47 = bf16[256,1024]{1,0:T(8,128)(2,1)S(1)} collective-permute-done((bf16[256,1024]{1,0:T(8,128)(2,1)S(1)}, bf16[256,1024]{1,0:T(8,128)(2,1)S(1)}, u32[]{:S(2)}, u32[]{:S(2)}) %collective-permute-start.47) | collective-permute-done | bytes 524320 | tf_op jit(solution)/shard_map/ppermute | solution.py:232
  279.1 1.5 fusion.107
  283.3 11.7 %collective-permute-done.52 = bf16[256,1024]{1,0:T(8,128)(2,1)} collective-permute-done((bf16[256,1024]{1,0:T(8,128)(2,1)S(1)}, bf16[256,1024]{1,0:T(8,128)(2,1)}, u32[]{:S(2)}, u32[]{:S(2)}) %collective-permute-start.52) | collective-permute-done | bytes 524320 | tf_op jit(solution)/shard_map/ppermute | solution.py:232
  295.0 7.7 %convolution_convert_fusion.9 = bf16[256,1024]{1,0:T(8,128)(2,1)} fusion(bf16[256,1024]{1,0:T(8,128)(2,1)} %collective-permute-done.52, f32[256,2048]{1,0:T(8,128)} %copy-done.90, bf16[1024,1024]{1,0:T(8,128)(2,1)} %copy-done.37, bf16[1024,1024]{1,0:T(8,128)(2,1)} %get-tuple-element.62, bf16[1024,1024]{1,0:T(8,128)(2,1)} %copy-done.36, ...), kind=kOutput, calls=%fused_computation.102 | convolution fusion | flops 2170814464 | bytes 11534336 | tf_op jit(solution)/shard_map/dot_general | solution.py:27
  303.3 11.0 %collective-permute-done.53 = bf16[256,1024]{1,0:T(8,128)(2,1)} collective-permute-done((bf16[256,1024]{1,0:T(8,128)(2,1)}, bf16[256,1024]{1,0:T(8,128)(2,1)}, u32[]{:S(2)}, u32[]{:S(2)}) %collective-permute-start.53) | collective-permute-done | bytes 524320 | tf_op jit(solution)/shard_map/ppermute | solution.py:232
  314.4 9.6 %fusion.99 = (f32[256]{0:T(256)S(1)}, f32[256]{0:T(256)S(1)}, f32[256,1024]{1,0:T(8,128)}) fusion(f32[256]{0:T(256)S(1)} %add_rsqrt_fusion.1, f32[256,1024]{1,0:T(8,128)} %copy-done.31, f32[256]{0:T(256)S(1)} %broadcast_multiply_fusion.9, f32[1024]{0:T(1024)S(1)} %bitcast.182, bf16[256,1024]{1,0:T(8,128)(2,1)} %collective-permute-done.53, ...), kind=kOutput, calls=%fused_computation.277 | convolution fusion | flops 2177367552 | bytes 14696448 | tf_op jit(solution)/shard_map/dot_general | solution.py:27
  323.9 2.0 fusion.101
  327.1 9.3 %collective-permute-done.54 = bf16[256,1024]{1,0:T(8,128)(2,1)S(1)} collective-permute-done((bf16[256,1024]{1,0:T(8,128)(2,1)S(1)}, bf16[256,1024]{1,0:T(8,128)(2,1)S(1)}, u32[]{:S(2)}, u32[]{:S(2)}) %collective-permute-start.54) | collective-permute-done | bytes 524320 | tf_op jit(solution)/shard_map/ppermute | solution.py:232
  336.9 14.5 %attend_back.2 = (bf16[512,512]{1,0:T(8,128)(2,1)S(1)}, f32[512,512]{1,0:T(8,128)S(1)}, f32[512,512]{1,0:T(8,128)S(1)}, bf16[512,512]{1,0:T(8,128)(2,1)S(1)}, bf...) custom-call(bf16[512,1536]{1,0:T(8,128)(2,1)S(1)} %pad_maximum_fusion.5.q.ko.vo, ...), custom_call_target="tpu_custom_call" | custom-call | flops 2852126720 | bytes 8388608 | tf_op jit(solution)/shard_map/attend_back/pallas_call | solution.py:161
  351.7 2.6 collective-permute-done.55
  355.3 1.8 copy-done.65
  358.7 13.4 %collective-permute-done.56 = bf16[256,1024]{1,0:T(8,128)(2,1)S(1)} collective-permute-done((bf16[256,1024]{1,0:T(8,128)(2,1)S(1)}, bf16[256,1024]{1,0:T(8,128)(2,1)S(1)}, u32[]{:S(2)}, u32[]{:S(2)}) %collective-permute-start.56) | collective-permute-done | bytes 524320 | tf_op jit(solution)/shard_map/ppermute | solution.py:232
  374.4 12.7 %collective-permute-done.57 = bf16[256,1024]{1,0:T(8,128)(2,1)} collective-permute-done((bf16[256,1024]{1,0:T(8,128)(2,1)S(1)}, bf16[256,1024]{1,0:T(8,128)(2,1)}, u32[]{:S(2)}, u32[]{:S(2)}) %collective-permute-start.57) | collective-permute-done | bytes 524320 | tf_op jit(solution)/shard_map/ppermute | solution.py:232
  387.1 7.7 %convolution_convert_fusion.7 = bf16[256,1024]{1,0:T(8,128)(2,1)} fusion(bf16[256,1024]{1,0:T(8,128)(2,1)} %collective-permute-done.57, f32[256,2048]{1,0:T(8,128)} %copy-done.88, bf16[1024,1024]{1,0:T(8,128)(2,1)} %copy-done.35, bf16[1024,1024]{1,0:T(8,128)(2,1)} %copy-done.43, bf16[1024,1024]{1,0:T(8,128)(2,1)} %copy-done.34, ...), kind=kOutput, calls=%fused_computation.100 | convolution fusion | flops 2170814464 | bytes 11534336 | tf_op jit(solution)/shard_map/dot_general | solution.py:27
  395.3 12.0 %collective-permute-done.58 = bf16[256,1024]{1,0:T(8,128)(2,1)} collective-permute-done((bf16[256,1024]{1,0:T(8,128)(2,1)}, bf16[256,1024]{1,0:T(8,128)(2,1)}, u32[]{:S(2)}, u32[]{:S(2)}) %collective-permute-start.58) | collective-permute-done | bytes 524320 | tf_op jit(solution)/shard_map/ppermute | solution.py:232
  407.3 9.3 %fusion.98 = (f32[256]{0:T(256)}, f32[256]{0:T(256)}, f32[256,1024]{1,0:T(8,128)}) fusion(f32[256]{0:T(256)} %copy-done.77, f32[256,1024]{1,0:T(8,128)} %copy-done.30, f32[256]{0:T(256)} %copy-done.73, f32[1024]{0:T(1024)S(1)} %bitcast.179, bf16[256,1024]{1,0:T(8,128)(2,1)} %collective-permute-done.58, bf16[1024,1024]{1,0:T(8,128)(2,1)} %copy-done.34, ...), kind=kOutput, calls=%fused_computation.276 | convolution fusion | flops 2177367552 | bytes 14696448 | tf_op jit(solution)/shard_map/dot_general | solution.py:27
  418.0 1.9 fusion.100
  421.1 10.2 %collective-permute-done.59 = bf16[256,1024]{1,0:T(8,128)(2,1)S(1)} collective-permute-done((bf16[256,1024]{1,0:T(8,128)(2,1)S(1)}, bf16[256,1024]{1,0:T(8,128)(2,1)S(1)}, u32[]{:S(2)}, u32[]{:S(2)}) %collective-permute-start.59) | collective-permute-done | bytes 524320 | tf_op jit(solution)/shard_map/ppermute | solution.py:232
  431.9 14.6 %attend_back.3 = (bf16[512,512]{1,0:T(8,128)(2,1)S(1)}, f32[512,512]{1,0:T(8,128)S(1)}, f32[512,512]{1,0:T(8,128)S(1)}, bf16[512,512]{1,0:T(8,128)(2,1)S(1)}, bf...) custom-call(bf16[512,1536]{1,0:T(8,128)(2,1)S(1)} %pad_maximum_fusion.4.q.ko.vo, ...), custom_call_target="tpu_custom_call" | custom-call | flops 2852126720 | bytes 8388608 | tf_op jit(solution)/shard_map/attend_back/pallas_call | solution.py:161
  447.3 2.0 collective-permute-done.60
  450.2 1.8 copy-done.33
  452.0 1.8 convolution_convert_fusion.6
  456.8 5.7 %collective-permute-start.48 = (bf16[256,1024]{1,0:T(8,128)(2,1)}, bf16[256,1024]{1,0:T(8,128)(2,1)S(1)}, u32[]{:S(2)}, u32[]{:S(2)}) collective-permute-start(bf16[256,1024]{1,0:T(8,128)(2,1)} %get-tuple-element.69), channel_id=1, source_target_pairs={{0,16},{1,17},{2,18},{3,19},{4,20},{5,21},{6,22},{7,23},{8,24},{9,... | collective-permute-start | bytes 1572872 | tf_op jit(solution)/shard_map/ppermute | solution.py:217
  463.2 4.9 collective-permute-done.61
  469.4 3.1 fusion.112
  472.5 1.6 collective-permute-start.67
  476.0 1.6 collective-permute-done.67
  477.6 2.6 collective-permute-start.68
  481.2 4.9 collective-permute-done.68
  (388 shorter events, 90.4 us)
Async XLA Ops:
  0.6 18.1 %collective-permute-start.18 = (bf16[1,1024]{1,0:T(2,128)(2,1)}, bf16[1,1024]{1,0:T(2,128)(2,1)}, u32[]{:S(2)}, u32[]{:S(2)}) collective-permute-start(bf16[1,1024]{1,0:T(2,128)(2,1)} %param.17), channel_id=1, source_target_pairs={{0,1},{1,0},{2,3},{3,2},{4,5},{5,4},{6,7},{7,6},{8,9},{9,8},{10,11... | collective-permute-start | bytes 6152 | tf_op jit(solution)/shard_map/ppermute | solution.py:223
  5.5 15.9 %collective-permute-start.40 = (bf16[1,1024]{1,0:T(2,128)(2,1)}, bf16[1,1024]{1,0:T(2,128)(2,1)}, u32[]{:S(2)}, u32[]{:S(2)}) collective-permute-start(bf16[1,1024]{1,0:T(2,128)(2,1)} %param.17), channel_id=1, source_target_pairs={{16,0},{17,1},{18,2},{19,3},{20,4},{21,5},{22,6},{23,7},{24,8},{25... | collective-permute-start | bytes 6152 | tf_op jit(solution)/shard_map/ppermute | solution.py:217
  6.8 16.0 %collective-permute-start.17 = (bf16[1,1024]{1,0:T(2,128)(2,1)}, bf16[1,1024]{1,0:T(2,128)(2,1)}, u32[]{:S(2)}, u32[]{:S(2)}) collective-permute-start(bf16[1,1024]{1,0:T(2,128)(2,1)} %param.17), channel_id=1, source_target_pairs={{0,16},{1,17},{2,18},{3,19},{4,20},{5,21},{6,22},{7,23},{8,24},{9,... | collective-permute-start | bytes 6152 | tf_op jit(solution)/shard_map/ppermute | solution.py:217
  11.0 44.9 %collective-permute-start.2 = (bf16[3,1024,256]{2,1,0:T(8,128)(2,1)}, bf16[3,1024,256]{2,1,0:T(8,128)(2,1)S(1)}, u32[]{:S(2)}, u32[]{:S(2)}) collective-permute-start(bf16[3,1024,256]{2,1,0:T(8,128)(2,1)} %bitcast.155), channel_id=1, source_target_pairs={{0,1},{1,0},{2,3},{3,2},{4,5},{5,4},{6,7},{7,6},{8,9},{9,8},{10,11... | collective-permute-start | bytes 4718600 | tf_op jit(solution)/shard_map/ppermute | solution.py:223
  12.9 48.1 %collective-permute-start.26 = (bf16[3,1024,256]{2,1,0:T(8,128)(2,1)}, bf16[3,1024,256]{2,1,0:T(8,128)(2,1)S(1)}, u32[]{:S(2)}, u32[]{:S(2)}) collective-permute-start(bf16[3,1024,256]{2,1,0:T(8,128)(2,1)} %bitcast.156), channel_id=1, source_target_pairs={{16,17},{17,16},{18,19},{19,18},{20,21},{21,20},{22,23},{23,22},{2... | collective-permute-start | bytes 4718600 | tf_op jit(solution)/shard_map/ppermute | solution.py:223
  18.7 7.3 %collective-permute-start.19 = (bf16[1,1024]{1,0:T(2,128)(2,1)}, bf16[1,1024]{1,0:T(2,128)(2,1)}, u32[]{:S(2)}, u32[]{:S(2)}) collective-permute-start(bf16[1,1024]{1,0:T(2,128)(2,1)} %collective-permute-done.18), channel_id=1, source_target_pairs={{0,16},{1,17},{2,18},{3,19},{4,20},{5,21},{6,22},{7,23},{8,24},{9,... | collective-permute-start | bytes 6152 | tf_op jit(solution)/shard_map/ppermute | solution.py:217
  21.4 43.4 %collective-permute-start.25 = (bf16[3,1024,256]{2,1,0:T(8,128)(2,1)}, bf16[3,1024,256]{2,1,0:T(8,128)(2,1)S(1)}, u32[]{:S(2)}, u32[]{:S(2)}) collective-permute-start(bf16[3,1024,256]{2,1,0:T(8,128)(2,1)} %bitcast.157), channel_id=1, source_target_pairs={{16,0},{17,1},{18,2},{19,3},{20,4},{21,5},{22,6},{23,7},{24,8},{25... | collective-permute-start | bytes 4718600 | tf_op jit(solution)/shard_map/ppermute | solution.py:217
  22.8 45.6 %collective-permute-start.1 = (bf16[3,1024,256]{2,1,0:T(8,128)(2,1)}, bf16[3,1024,256]{2,1,0:T(8,128)(2,1)S(1)}, u32[]{:S(2)}, u32[]{:S(2)}) collective-permute-start(bf16[3,1024,256]{2,1,0:T(8,128)(2,1)} %bitcast.158), channel_id=1, source_target_pairs={{0,16},{1,17},{2,18},{3,19},{4,20},{5,21},{6,22},{7,23},{8,24},{9,... | collective-permute-start | bytes 4718600 | tf_op jit(solution)/shard_map/ppermute | solution.py:217
  28.8 3.3 collective-permute-start.30
  32.1 17.5 %collective-permute-start.7 = (bf16[2,64,256]{2,1,0:T(8,128)(2,1)}, bf16[2,64,256]{2,1,0:T(8,128)(2,1)S(1)}, u32[]{:S(2)}, u32[]{:S(2)}) collective-permute-start(bf16[2,64,256]{2,1,0:T(8,128)(2,1)} %bitcast.160), channel_id=1, source_target_pairs={{0,1},{1,0},{2,3},{3,2},{4,5},{5,4},{6,7},{7,6},{8,9},{9,8},{10,11... | collective-permute-start | bytes 196616 | tf_op jit(solution)/shard_map/ppermute | solution.py:223
  52.0 3.1 collective-permute-start.8
  55.2 7.1 %collective-permute-start = (bf16[256,1024]{1,0:T(8,128)(2,1)}, bf16[256,1024]{1,0:T(8,128)(2,1)S(1)}, u32[]{:S(2)}, u32[]{:S(2)}) collective-permute-start(bf16[256,1024]{1,0:T(8,128)(2,1)} %dynamic-slice_bitcast_fusion.1), channel_id=1, source_target_pairs={{16,17},{17,16},{18,19},{19,18},{20,21},{21,20},{22,23},{23,22},{2... | collective-permute-start | bytes 1572872 | tf_op jit(solution)/shard_map/ppermute | solution.py:223
  55.9 15.3 %collective-permute-start.3 = (bf16[3,1024,256]{2,1,0:T(8,128)(2,1)S(1)}, bf16[3,1024,256]{2,1,0:T(8,128)(2,1)S(1)}, u32[]{:S(2)}, u32[]{:S(2)}) collective-permute-start(bf16[3,1024,256]{2,1,0:T(8,128)(2,1)S(1)} %collective-permute-done.2), channel_id=1, source_target_pairs={{0,16},{1,17},{2,18},{3,19},{4,20},{5,21},{6,22},{7,23},{8,24},{9,... | collective-permute-start | bytes 4718600 | tf_op jit(solution)/shard_map/ppermute | solution.py:217
  61.0 13.1 %collective-permute-start.27 = (bf16[3,1024,256]{2,1,0:T(8,128)(2,1)S(1)}, bf16[3,1024,256]{2,1,0:T(8,128)(2,1)S(1)}, u32[]{:S(2)}, u32[]{:S(2)}) collective-permute-start(bf16[3,1024,256]{2,1,0:T(8,128)(2,1)S(1)} %collective-permute-done.26), channel_id=1, source_target_pairs={{16,0},{17,1},{18,2},{19,3},{20,4},{21,5},{22,6},{23,7},{24,8},{25... | collective-permute-start | bytes 4718600 | tf_op jit(solution)/shard_map/ppermute | solution.py:217
  62.3 15.5 %collective-permute-start.33 = (bf16[256,1024]{1,0:T(8,128)(2,1)}, bf16[256,1024]{1,0:T(8,128)(2,1)S(1)}, u32[]{:S(2)}, u32[]{:S(2)}) collective-permute-start(bf16[256,1024]{1,0:T(8,128)(2,1)} %bitcast.17), channel_id=1, source_target_pairs={{16,0},{17,1},{18,2},{19,3},{20,4},{21,5},{22,6},{23,7},{24,8},{25... | collective-permute-start | bytes 1572872 | tf_op jit(solution)/shard_map/ppermute | solution.py:217
  64.8 14.7 %collective-permute-start.10 = (bf16[256,1024]{1,0:T(8,128)(2,1)}, bf16[256,1024]{1,0:T(8,128)(2,1)S(1)}, u32[]{:S(2)}, u32[]{:S(2)}) collective-permute-start(bf16[256,1024]{1,0:T(8,128)(2,1)} %bitcast.17), channel_id=1, source_target_pairs={{0,1},{1,0},{2,3},{3,2},{4,5},{5,4},{6,7},{7,6},{8,9},{9,8},{10,11... | collective-permute-start | bytes 1572872 | tf_op jit(solution)/shard_map/ppermute | solution.py:223
  68.4 12.4 %collective-permute-start.9 = (bf16[256,1024]{1,0:T(8,128)(2,1)}, bf16[256,1024]{1,0:T(8,128)(2,1)S(1)}, u32[]{:S(2)}, u32[]{:S(2)}) collective-permute-start(bf16[256,1024]{1,0:T(8,128)(2,1)} %bitcast.17), channel_id=1, source_target_pairs={{0,16},{1,17},{2,18},{3,19},{4,20},{5,21},{6,22},{7,23},{8,24},{9,... | collective-permute-start | bytes 1572872 | tf_op jit(solution)/shard_map/ppermute | solution.py:217
  72.6 21.9 %collective-permute-start.37 = (bf16[1024,1024]{1,0:T(8,128)(2,1)S(1)}, bf16[1024,1024]{1,0:T(8,128)(2,1)S(1)}, u32[]{:S(2)}, u32[]{:S(2)}) collective-permute-start(bf16[1024,1024]{1,0:T(8,128)(2,1)S(1)} %bitcast.147), channel_id=1, source_target_pairs={{16,0},{17,1},{18,2},{19,3},{20,4},{21,5},{22,6},{23,7},{24,8},{25... | collective-permute-start | bytes 6291464 | tf_op jit(solution)/shard_map/ppermute | solution.py:217
  74.1 24.6 %collective-permute-start.14 = (bf16[1024,1024]{1,0:T(8,128)(2,1)S(1)}, bf16[1024,1024]{1,0:T(8,128)(2,1)S(1)}, u32[]{:S(2)}, u32[]{:S(2)}) collective-permute-start(bf16[1024,1024]{1,0:T(8,128)(2,1)S(1)} %bitcast.148), channel_id=1, source_target_pairs={{0,16},{1,17},{2,18},{3,19},{4,20},{5,21},{6,22},{7,23},{8,24},{9,... | collective-permute-start | bytes 6291464 | tf_op jit(solution)/shard_map/ppermute | solution.py:217
  77.9 13.1 %collective-permute-start.4 = (bf16[256,1024]{1,0:T(8,128)(2,1)S(1)}, bf16[256,1024]{1,0:T(8,128)(2,1)S(1)}, u32[]{:S(2)}, u32[]{:S(2)}) collective-permute-start(bf16[256,1024]{1,0:T(8,128)(2,1)S(1)} %bitcast_select_fusion.1), channel_id=1, source_target_pairs={{2,0},{3,1},{0,2},{1,3},{6,4},{7,5},{4,6},{5,7},{10,8},{11,9},{8,1... | collective-permute-start | bytes 1572872 | tf_op jit(solution)/shard_map/ppermute | solution.py:232
  79.5 12.9 %collective-permute-start.11 = (bf16[256,1024]{1,0:T(8,128)(2,1)S(1)}, bf16[256,1024]{1,0:T(8,128)(2,1)S(1)}, u32[]{:S(2)}, u32[]{:S(2)}) collective-permute-start(bf16[256,1024]{1,0:T(8,128)(2,1)S(1)} %collective-permute-done.10), channel_id=1, source_target_pairs={{0,16},{1,17},{2,18},{3,19},{4,20},{5,21},{6,22},{7,23},{8,24},{9,... | collective-permute-start | bytes 1572872 | tf_op jit(solution)/shard_map/ppermute | solution.py:217
  80.9 28.6 %collective-permute-start.15 = (bf16[1024,1024]{1,0:T(8,128)(2,1)S(1)}, bf16[1024,1024]{1,0:T(8,128)(2,1)S(1)}, u32[]{:S(2)}, u32[]{:S(2)}) collective-permute-start(bf16[1024,1024]{1,0:T(8,128)(2,1)S(1)} %bitcast.149), channel_id=1, source_target_pairs={{0,1},{1,0},{2,3},{3,2},{4,5},{5,4},{6,7},{7,6},{8,9},{9,8},{10,11... | collective-permute-start | bytes 6291464 | tf_op jit(solution)/shard_map/ppermute | solution.py:223
  91.0 33.8 %collective-permute-start.43 = (bf16[1024,1024]{1,0:T(8,128)(2,1)S(1)}, bf16[1024,1024]{1,0:T(8,128)(2,1)S(1)}, u32[]{:S(2)}, u32[]{:S(2)}) collective-permute-start(bf16[1024,1024]{1,0:T(8,128)(2,1)S(1)} %bitcast.151), channel_id=1, source_target_pairs={{16,0},{17,1},{18,2},{19,3},{20,4},{21,5},{22,6},{23,7},{24,8},{25... | collective-permute-start | bytes 6291464 | tf_op jit(solution)/shard_map/ppermute | solution.py:217
  92.3 55.9 %collective-permute-start.21 = (bf16[1024,1024]{1,0:T(8,128)(2,1)S(1)}, bf16[1024,1024]{1,0:T(8,128)(2,1)S(1)}, u32[]{:S(2)}, u32[]{:S(2)}) collective-permute-start(bf16[1024,1024]{1,0:T(8,128)(2,1)S(1)} %bitcast.152), channel_id=1, source_target_pairs={{0,1},{1,0},{2,3},{3,2},{4,5},{5,4},{6,7},{7,6},{8,9},{9,8},{10,11... | collective-permute-start | bytes 6291464 | tf_op jit(solution)/shard_map/ppermute | solution.py:223
  94.6 55.1 %collective-permute-start.20 = (bf16[1024,1024]{1,0:T(8,128)(2,1)S(1)}, bf16[1024,1024]{1,0:T(8,128)(2,1)}, u32[]{:S(2)}, u32[]{:S(2)}) collective-permute-start(bf16[1024,1024]{1,0:T(8,128)(2,1)S(1)} %bitcast.153), channel_id=1, source_target_pairs={{0,16},{1,17},{2,18},{3,19},{4,20},{5,21},{6,22},{7,23},{8,24},{9,... | collective-permute-start | bytes 6291464 | tf_op jit(solution)/shard_map/ppermute | solution.py:217
  98.7 11.5 %collective-permute-start.5 = (bf16[512,1024]{1,0:T(8,128)(2,1)S(1)}, bf16[512,1024]{1,0:T(8,128)(2,1)S(1)}, u32[]{:S(2)}, u32[]{:S(2)}) collective-permute-start(bf16[512,1024]{1,0:T(8,128)(2,1)S(1)} %fusion.41), channel_id=1, source_target_pairs={{0,16},{16,0},{1,17},{17,1},{2,18},{18,2},{3,19},{19,3},{4,20},{20... | collective-permute-start | bytes 3145736 | tf_op jit(solution)/shard_map/ppermute | solution.py:217
  109.5 44.4 %collective-permute-start.34 = (bf16[256,1024]{1,0:T(8,128)(2,1)}, bf16[256,1024]{1,0:T(8,128)(2,1)S(1)}, u32[]{:S(2)}, u32[]{:S(2)}) collective-permute-start(bf16[256,1024]{1,0:T(8,128)(2,1)} %bitcast.17), channel_id=1, source_target_pairs={{16,17},{17,16},{18,19},{19,18},{20,21},{21,20},{22,23},{23,22},{2... | collective-permute-start | bytes 1572872 | tf_op jit(solution)/shard_map/ppermute | solution.py:223
  110.2 51.2 %collective-permute-start.16 = (bf16[1024,1024]{1,0:T(8,128)(2,1)S(1)}, bf16[1024,1024]{1,0:T(8,128)(2,1)S(1)}, u32[]{:S(2)}, u32[]{:S(2)}) collective-permute-start(bf16[1024,1024]{1,0:T(8,128)(2,1)S(1)} %collective-permute-done.15), channel_id=1, source_target_pairs={{0,16},{1,17},{2,18},{3,19},{4,20},{5,21},{6,22},{7,23},{8,24},{9,... | collective-permute-start | bytes 6291464 | tf_op jit(solution)/shard_map/ppermute | solution.py:217
  124.8 92.0 %collective-permute-start.38 = (bf16[1024,1024]{1,0:T(8,128)(2,1)S(1)}, bf16[1024,1024]{1,0:T(8,128)(2,1)S(1)}, u32[]{:S(2)}, u32[]{:S(2)}) collective-permute-start(bf16[1024,1024]{1,0:T(8,128)(2,1)S(1)} %bitcast.150), channel_id=1, source_target_pairs={{16,17},{17,16},{18,19},{19,18},{20,21},{21,20},{22,23},{23,22},{2... | collective-permute-start | bytes 6291464 | tf_op jit(solution)/shard_map/ppermute | solution.py:223
  148.2 13.5 %collective-permute-start.22 = (bf16[1024,1024]{1,0:T(8,128)(2,1)S(1)}, bf16[1024,1024]{1,0:T(8,128)(2,1)S(1)}, u32[]{:S(2)}, u32[]{:S(2)}) collective-permute-start(bf16[1024,1024]{1,0:T(8,128)(2,1)S(1)} %collective-permute-done.21), channel_id=1, source_target_pairs={{0,16},{1,17},{2,18},{3,19},{4,20},{5,21},{6,22},{7,23},{8,24},{9,... | collective-permute-start | bytes 6291464 | tf_op jit(solution)/shard_map/ppermute | solution.py:217
  149.6 9.2 %collective-permute-start.12 = (bf16[256,1024]{1,0:T(8,128)(2,1)S(1)}, bf16[256,1024]{1,0:T(8,128)(2,1)S(1)}, u32[]{:S(2)}, u32[]{:S(2)}) collective-permute-start(bf16[256,1024]{1,0:T(8,128)(2,1)S(1)} %convolution_convert_fusion.5), channel_id=1, source_target_pairs={{2,0},{3,1},{0,2},{1,3},{6,4},{7,5},{4,6},{5,7},{10,8},{11,9},{8,1... | collective-permute-start | bytes 1572872 | tf_op jit(solution)/shard_map/ppermute | solution.py:232
  153.9 64.2 %collective-permute-start.44 = (bf16[1024,1024]{1,0:T(8,128)(2,1)S(1)}, bf16[1024,1024]{1,0:T(8,128)(2,1)S(1)}, u32[]{:S(2)}, u32[]{:S(2)}) collective-permute-start(bf16[1024,1024]{1,0:T(8,128)(2,1)S(1)} %bitcast.154), channel_id=1, source_target_pairs={{16,17},{17,16},{18,19},{19,18},{20,21},{21,20},{22,23},{23,22},{2... | collective-permute-start | bytes 6291464 | tf_op jit(solution)/shard_map/ppermute | solution.py:223
  158.9 57.9 %collective-permute-start.35 = (bf16[256,1024]{1,0:T(8,128)(2,1)S(1)}, bf16[256,1024]{1,0:T(8,128)(2,1)S(1)}, u32[]{:S(2)}, u32[]{:S(2)}) collective-permute-start(bf16[256,1024]{1,0:T(8,128)(2,1)S(1)} %collective-permute-done.34), channel_id=1, source_target_pairs={{16,0},{17,1},{18,2},{19,3},{20,4},{21,5},{22,6},{23,7},{24,8},{25... | collective-permute-start | bytes 1572872 | tf_op jit(solution)/shard_map/ppermute | solution.py:217
  161.4 14.7 %collective-permute-start.23 = (bf16[256,1024]{1,0:T(8,128)(2,1)S(1)}, bf16[256,1024]{1,0:T(8,128)(2,1)S(1)}, u32[]{:S(2)}, u32[]{:S(2)}) collective-permute-start(bf16[256,1024]{1,0:T(8,128)(2,1)S(1)} %fusion.48), channel_id=1, source_target_pairs={{2,0},{3,1},{0,2},{1,3},{6,4},{7,5},{4,6},{5,7},{10,8},{11,9},{8,1... | collective-permute-start | bytes 1572872 | tf_op jit(solution)/shard_map/ppermute | solution.py:232
  178.6 14.0 %collective-permute-start.24 = (bf16[256,1024]{1,0:T(8,128)(2,1)S(1)}, bf16[256,1024]{1,0:T(8,128)(2,1)S(1)}, u32[]{:S(2)}, u32[]{:S(2)}) collective-permute-start(bf16[256,1024]{1,0:T(8,128)(2,1)S(1)} %convolution_convert_fusion.11), channel_id=1, source_target_pairs={{2,0},{3,1},{0,2},{1,3},{6,4},{7,5},{4,6},{5,7},{10,8},{11,9},{8,1... | collective-permute-start | bytes 1572872 | tf_op jit(solution)/shard_map/ppermute | solution.py:232
  194.8 13.2 %collective-permute-start.28 = (bf16[256,1024]{1,0:T(8,128)(2,1)S(1)}, bf16[256,1024]{1,0:T(8,128)(2,1)S(1)}, u32[]{:S(2)}, u32[]{:S(2)}) collective-permute-start(bf16[256,1024]{1,0:T(8,128)(2,1)S(1)} %add_convert_fusion.1), channel_id=1, source_target_pairs={{2,0},{3,1},{0,2},{1,3},{6,4},{7,5},{4,6},{5,7},{10,8},{11,9},{8,1... | collective-permute-start | bytes 1572872 | tf_op jit(solution)/shard_map/ppermute | solution.py:232
  209.1 10.9 %collective-permute-start.29 = (bf16[512,1024]{1,0:T(8,128)(2,1)S(1)}, bf16[512,1024]{1,0:T(8,128)(2,1)S(1)}, u32[]{:S(2)}, u32[]{:S(2)}) collective-permute-start(bf16[512,1024]{1,0:T(8,128)(2,1)S(1)} %fusion.40), channel_id=1, source_target_pairs={{0,16},{16,0},{1,17},{17,1},{2,18},{18,2},{3,19},{19,3},{4,20},{20... | collective-permute-start | bytes 3145736 | tf_op jit(solution)/shard_map/ppermute | solution.py:217
  210.4 6.3 %collective-permute-start.32 = (bf16[2,64,256]{2,1,0:T(8,128)(2,1)S(1)}, bf16[2,64,256]{2,1,0:T(8,128)(2,1)S(1)}, u32[]{:S(2)}, u32[]{:S(2)}) collective-permute-start(bf16[2,64,256]{2,1,0:T(8,128)(2,1)S(1)} %collective-permute-done.31), channel_id=1, source_target_pairs={{16,0},{17,1},{18,2},{19,3},{20,4},{21,5},{22,6},{23,7},{24,8},{25... | collective-permute-start | bytes 196616 | tf_op jit(solution)/shard_map/ppermute | solution.py:217
  216.9 32.7 %collective-permute-start.39 = (bf16[1024,1024]{1,0:T(8,128)(2,1)S(1)}, bf16[1024,1024]{1,0:T(8,128)(2,1)S(1)}, u32[]{:S(2)}, u32[]{:S(2)}) collective-permute-start(bf16[1024,1024]{1,0:T(8,128)(2,1)S(1)} %collective-permute-done.38), channel_id=1, source_target_pairs={{16,0},{17,1},{18,2},{19,3},{20,4},{21,5},{22,6},{23,7},{24,8},{25... | collective-permute-start | bytes 6291464 | tf_op jit(solution)/shard_map/ppermute | solution.py:217
  218.2 31.7 %collective-permute-start.45 = (bf16[1024,1024]{1,0:T(8,128)(2,1)S(1)}, bf16[1024,1024]{1,0:T(8,128)(2,1)S(1)}, u32[]{:S(2)}, u32[]{:S(2)}) collective-permute-start(bf16[1024,1024]{1,0:T(8,128)(2,1)S(1)} %collective-permute-done.44), channel_id=1, source_target_pairs={{16,0},{17,1},{18,2},{19,3},{20,4},{21,5},{22,6},{23,7},{24,8},{25... | collective-permute-start | bytes 6291464 | tf_op jit(solution)/shard_map/ppermute | solution.py:217
  233.2 14.5 %collective-permute-start.36 = (bf16[256,1024]{1,0:T(8,128)(2,1)S(1)}, bf16[256,1024]{1,0:T(8,128)(2,1)S(1)}, u32[]{:S(2)}, u32[]{:S(2)}) collective-permute-start(bf16[256,1024]{1,0:T(8,128)(2,1)S(1)} %convolution_convert_fusion.4), channel_id=1, source_target_pairs={{2,0},{3,1},{0,2},{1,3},{6,4},{7,5},{4,6},{5,7},{10,8},{11,9},{8,1... | collective-permute-start | bytes 1572872 | tf_op jit(solution)/shard_map/ppermute | solution.py:232
  234.6 7.0 %collective-permute-start.42 = (bf16[1,1024]{1,0:T(2,128)(2,1)S(1)}, bf16[1,1024]{1,0:T(2,128)(2,1)S(1)}, u32[]{:S(2)}, u32[]{:S(2)}) collective-permute-start(bf16[1,1024]{1,0:T(2,128)(2,1)S(1)} %collective-permute-done.41), channel_id=1, source_target_pairs={{16,0},{17,1},{18,2},{19,3},{20,4},{21,5},{22,6},{23,7},{24,8},{25... | collective-permute-start | bytes 6152 | tf_op jit(solution)/shard_map/ppermute | solution.py:217
  248.9 14.1 %collective-permute-start.46 = (bf16[256,1024]{1,0:T(8,128)(2,1)S(1)}, bf16[256,1024]{1,0:T(8,128)(2,1)S(1)}, u32[]{:S(2)}, u32[]{:S(2)}) collective-permute-start(bf16[256,1024]{1,0:T(8,128)(2,1)S(1)} %fusion.49), channel_id=1, source_target_pairs={{2,0},{3,1},{0,2},{1,3},{6,4},{7,5},{4,6},{5,7},{10,8},{11,9},{8,1... | collective-permute-start | bytes 1572872 | tf_op jit(solution)/shard_map/ppermute | solution.py:232
  265.9 13.2 %collective-permute-start.47 = (bf16[256,1024]{1,0:T(8,128)(2,1)S(1)}, bf16[256,1024]{1,0:T(8,128)(2,1)S(1)}, u32[]{:S(2)}, u32[]{:S(2)}) collective-permute-start(bf16[256,1024]{1,0:T(8,128)(2,1)S(1)} %convolution_convert_fusion.10), channel_id=1, source_target_pairs={{2,0},{3,1},{0,2},{1,3},{6,4},{7,5},{4,6},{5,7},{10,8},{11,9},{8,1... | collective-permute-start | bytes 1572872 | tf_op jit(solution)/shard_map/ppermute | solution.py:232
  266.6 14.3 %collective-permute-start.51 = (bf16[256,1024]{1,0:T(8,128)(2,1)S(1)}, bf16[256,1024]{1,0:T(8,128)(2,1)S(1)}, u32[]{:S(2)}, u32[]{:S(2)}) collective-permute-start(bf16[256,1024]{1,0:T(8,128)(2,1)S(1)} %dynamic-slice_bitcast_fusion), channel_id=1, source_target_pairs={{16,17},{17,16},{18,19},{19,18},{20,21},{21,20},{22,23},{23,22},{2... | collective-permute-start | bytes 1572872 | tf_op jit(solution)/shard_map/ppermute | solution.py:223
  282.7 12.3 %collective-permute-start.52 = (bf16[256,1024]{1,0:T(8,128)(2,1)S(1)}, bf16[256,1024]{1,0:T(8,128)(2,1)}, u32[]{:S(2)}, u32[]{:S(2)}) collective-permute-start(bf16[256,1024]{1,0:T(8,128)(2,1)S(1)} %get-tuple-element.68), channel_id=1, source_target_pairs={{2,0},{3,1},{0,2},{1,3},{6,4},{7,5},{4,6},{5,7},{10,8},{11,9},{8,1... | collective-permute-start | bytes 1572872 | tf_op jit(solution)/shard_map/ppermute | solution.py:232
  302.7 11.6 %collective-permute-start.53 = (bf16[256,1024]{1,0:T(8,128)(2,1)}, bf16[256,1024]{1,0:T(8,128)(2,1)}, u32[]{:S(2)}, u32[]{:S(2)}) collective-permute-start(bf16[256,1024]{1,0:T(8,128)(2,1)} %convolution_convert_fusion.9), channel_id=1, source_target_pairs={{2,0},{3,1},{0,2},{1,3},{6,4},{7,5},{4,6},{5,7},{10,8},{11,9},{8,1... | collective-permute-start | bytes 1572872 | tf_op jit(solution)/shard_map/ppermute | solution.py:232
  325.9 10.5 %collective-permute-start.54 = (bf16[256,1024]{1,0:T(8,128)(2,1)S(1)}, bf16[256,1024]{1,0:T(8,128)(2,1)S(1)}, u32[]{:S(2)}, u32[]{:S(2)}) collective-permute-start(bf16[256,1024]{1,0:T(8,128)(2,1)S(1)} %get-tuple-element.51), channel_id=1, source_target_pairs={{2,0},{3,1},{0,2},{1,3},{6,4},{7,5},{4,6},{5,7},{10,8},{11,9},{8,1... | collective-permute-start | bytes 1572872 | tf_op jit(solution)/shard_map/ppermute | solution.py:232
  358.1 14.0 %collective-permute-start.56 = (bf16[256,1024]{1,0:T(8,128)(2,1)S(1)}, bf16[256,1024]{1,0:T(8,128)(2,1)S(1)}, u32[]{:S(2)}, u32[]{:S(2)}) collective-permute-start(bf16[256,1024]{1,0:T(8,128)(2,1)S(1)} %convolution_convert_fusion.8), channel_id=1, source_target_pairs={{2,0},{3,1},{0,2},{1,3},{6,4},{7,5},{4,6},{5,7},{10,8},{11,9},{8,1... | collective-permute-start | bytes 1572872 | tf_op jit(solution)/shard_map/ppermute | solution.py:232
  373.7 13.3 %collective-permute-start.57 = (bf16[256,1024]{1,0:T(8,128)(2,1)S(1)}, bf16[256,1024]{1,0:T(8,128)(2,1)}, u32[]{:S(2)}, u32[]{:S(2)}) collective-permute-start(bf16[256,1024]{1,0:T(8,128)(2,1)S(1)} %fusion.93), channel_id=1, source_target_pairs={{2,0},{3,1},{0,2},{1,3},{6,4},{7,5},{4,6},{5,7},{10,8},{11,9},{8,1... | collective-permute-start | bytes 1572872 | tf_op jit(solution)/shard_map/ppermute | solution.py:232
  394.8 12.5 %collective-permute-start.58 = (bf16[256,1024]{1,0:T(8,128)(2,1)}, bf16[256,1024]{1,0:T(8,128)(2,1)}, u32[]{:S(2)}, u32[]{:S(2)}) collective-permute-start(bf16[256,1024]{1,0:T(8,128)(2,1)} %convolution_convert_fusion.7), channel_id=1, source_target_pairs={{2,0},{3,1},{0,2},{1,3},{6,4},{7,5},{4,6},{5,7},{10,8},{11,9},{8,1... | collective-permute-start | bytes 1572872 | tf_op jit(solution)/shard_map/ppermute | solution.py:232
  419.9 11.4 %collective-permute-start.59 = (bf16[256,1024]{1,0:T(8,128)(2,1)S(1)}, bf16[256,1024]{1,0:T(8,128)(2,1)S(1)}, u32[]{:S(2)}, u32[]{:S(2)}) collective-permute-start(bf16[256,1024]{1,0:T(8,128)(2,1)S(1)} %get-tuple-element.49), channel_id=1, source_target_pairs={{2,0},{3,1},{0,2},{1,3},{6,4},{7,5},{4,6},{5,7},{10,8},{11,9},{8,1... | collective-permute-start | bytes 1572872 | tf_op jit(solution)/shard_map/ppermute | solution.py:232
  446.6 2.7 collective-permute-start.60
  446.7 7.7 %collective-permute-start.65 = (f32[2,64,512]{2,1,0:T(8,128)S(1)}, f32[2,64,512]{2,1,0:T(8,128)S(1)}, u32[]{:S(2)}, u32[]{:S(2)}) collective-permute-start(f32[2,64,512]{2,1,0:T(8,128)S(1)} %fusion.73), channel_id=1, source_target_pairs={{0,16},{16,0},{1,17},{17,1},{2,18},{18,2},{3,19},{19,3},{4,20},{20... | collective-permute-start | bytes 786440 | tf_op jit(solution)/shard_map/ppermute | solution.py:217
  453.8 14.3 %collective-permute-start.61 = (bf16[256,1024]{1,0:T(8,128)(2,1)}, bf16[256,1024]{1,0:T(8,128)(2,1)}, u32[]{:S(2)}, u32[]{:S(2)}) collective-permute-start(bf16[256,1024]{1,0:T(8,128)(2,1)} %convolution_convert_fusion.6), channel_id=1, source_target_pairs={{2,0},{3,1},{0,2},{1,3},{6,4},{7,5},{4,6},{5,7},{10,8},{11,9},{8,1... | collective-permute-start | bytes 1572872 | tf_op jit(solution)/shard_map/ppermute | solution.py:232
  454.4 8.0 %collective-permute-start.66 = (f32[2,64,256]{2,1,0:T(8,128)S(1)}, f32[2,64,256]{2,1,0:T(8,128)S(1)}, u32[]{:S(2)}, u32[]{:S(2)}) collective-permute-start(f32[2,64,256]{2,1,0:T(8,128)S(1)} %slice.246), channel_id=1, source_target_pairs={{0,1},{1,0},{2,3},{3,2},{4,5},{5,4},{6,7},{7,6},{8,9},{9,8},{10,11... | collective-permute-start | bytes 393224 | tf_op jit(solution)/shard_map/ppermute | solution.py:221
  454.8 17.7 %collective-permute-start.49 = (bf16[256,1024]{1,0:T(8,128)(2,1)}, bf16[256,1024]{1,0:T(8,128)(2,1)S(1)}, u32[]{:S(2)}, u32[]{:S(2)}) collective-permute-start(bf16[256,1024]{1,0:T(8,128)(2,1)} %copy-done.55), channel_id=1, source_target_pairs={{16,1},{17,0},{18,3},{19,2},{20,5},{21,4},{22,7},{23,6},{24,9},{25... | collective-permute-start | bytes 1572872 | tf_op jit(solution)/shard_map/ppermute | solution.py:227
  456.1 18.1 %collective-permute-start.50 = (bf16[256,1024]{1,0:T(8,128)(2,1)}, bf16[256,1024]{1,0:T(8,128)(2,1)S(1)}, u32[]{:S(2)}, u32[]{:S(2)}) collective-permute-start(bf16[256,1024]{1,0:T(8,128)(2,1)} %get-tuple-element.69), channel_id=1, source_target_pairs={{16,17},{17,16},{18,19},{19,18},{20,21},{21,20},{22,23},{23,22},{2... | collective-permute-start | bytes 1572872 | tf_op jit(solution)/shard_map/ppermute | solution.py:223
  456.8 18.6 %collective-permute-start.48 = (bf16[256,1024]{1,0:T(8,128)(2,1)}, bf16[256,1024]{1,0:T(8,128)(2,1)S(1)}, u32[]{:S(2)}, u32[]{:S(2)}) collective-permute-start(bf16[256,1024]{1,0:T(8,128)(2,1)} %get-tuple-element.69), channel_id=1, source_target_pairs={{0,16},{1,17},{2,18},{3,19},{4,20},{5,21},{6,22},{7,23},{8,24},{9,... | collective-permute-start | bytes 1572872 | tf_op jit(solution)/shard_map/ppermute | solution.py:217
  462.5 24.3 %collective-permute-start.64 = (bf16[256,1024]{1,0:T(8,128)(2,1)}, bf16[256,1024]{1,0:T(8,128)(2,1)S(1)}, u32[]{:S(2)}, u32[]{:S(2)}) collective-permute-start(bf16[256,1024]{1,0:T(8,128)(2,1)} %copy-done.58), channel_id=1, source_target_pairs={{16,17},{17,16},{18,19},{19,18},{20,21},{21,20},{22,23},{23,22},{2... | collective-permute-start | bytes 1572872 | tf_op jit(solution)/shard_map/ppermute | solution.py:223
  468.1 18.7 %collective-permute-start.62 = (bf16[256,1024]{1,0:T(8,128)(2,1)}, bf16[256,1024]{1,0:T(8,128)(2,1)S(1)}, u32[]{:S(2)}, u32[]{:S(2)}) collective-permute-start(bf16[256,1024]{1,0:T(8,128)(2,1)} %copy-done.58), channel_id=1, source_target_pairs={{0,16},{1,17},{2,18},{3,19},{4,20},{5,21},{6,22},{7,23},{8,24},{9,... | collective-permute-start | bytes 1572872 | tf_op jit(solution)/shard_map/ppermute | solution.py:217
  472.5 5.0 %collective-permute-start.67 = (f32[2,64,256]{2,1,0:T(8,128)S(1)}, f32[2,64,256]{2,1,0:T(8,128)S(1)}, u32[]{:S(2)}, u32[]{:S(2)}) collective-permute-start(f32[2,64,256]{2,1,0:T(8,128)S(1)} %slice_add_fusion.4), channel_id=1, source_target_pairs={{0,4},{4,0},{8,12},{12,8},{1,5},{5,1},{9,13},{13,9},{2,6},{6,2},{1... | collective-permute-start | bytes 393224 | tf_op jit(solution)/shard_map/ppermute | solution.py:308
  474.2 12.6 %collective-permute-start.63 = (bf16[256,1024]{1,0:T(8,128)(2,1)S(1)}, bf16[256,1024]{1,0:T(8,128)(2,1)S(1)}, u32[]{:S(2)}, u32[]{:S(2)}) collective-permute-start(bf16[256,1024]{1,0:T(8,128)(2,1)S(1)} %get-tuple-element.107), channel_id=1, source_target_pairs={{16,1},{17,0},{18,3},{19,2},{20,5},{21,4},{22,7},{23,6},{24,9},{25... | collective-permute-start | bytes 1572872 | tf_op jit(solution)/shard_map/ppermute | solution.py:227
  477.6 8.5 %collective-permute-start.68 = (f32[2,64,256]{2,1,0:T(8,128)S(1)}, f32[2,64,256]{2,1,0:T(8,128)S(1)}, u32[]{:S(2)}, u32[]{:S(2)}) collective-permute-start(f32[2,64,256]{2,1,0:T(8,128)S(1)} %add.348), channel_id=1, source_target_pairs={{0,8},{4,12},{8,0},{12,4},{1,9},{5,13},{9,1},{13,5},{2,10},{6,14},... | collective-permute-start | bytes 393224 | tf_op jit(solution)/shard_map/ppermute | solution.py:308
  (96 other events, 1891.2 us)

commit v2 on v1

--- a/solution.py
+++ b/solution.py
@@ -203,6 +203,785 @@
     return (u * cdf).astype(BF16), (cdf + u * pdf).astype(BF16)
 
 
+MESH = pl.DeviceIdType.MESH
+ROWS = 256
+CORE = 2 * ROWS
+CHUNK = 128
+STEPS = ROWS // CHUNK
+QUARTER = D // 4
+UNITS = D
+TILE = 256
+PAIRS = 4
+KEYS = 2 * CORE + PREFIX
+SEMS = 128
+
+
+def gelu_both(u):
+    size = jnp.abs(u) * 0.7071067811865476
+    t = 1.0 / (1.0 + 0.3275911 * size)
+    poly = t * (0.254829592 + t * (-0.284496736 + t * (1.421413741 + t * (-1.453152027 + t * 1.061405429))))
+    bell = jnp.exp(-(size * size))
+    tail = 0.5 * poly * bell
+    cdf = jnp.where(u >= 0, 1.0 - tail, tail)
+    return (u * cdf).astype(BF16), (cdf + u * (bell * 0.3989422804014327)).astype(BF16)
+
+
+def norm_chunk(values):
+    center = values - jnp.mean(values, axis=-1, keepdims=True)
+    scale = lax.rsqrt(jnp.mean(center * center, axis=-1, keepdims=True) + 1e-05)
+    return center * scale, scale
+
+
+class Copies:
+    def __init__(self, send, arrive, here):
+        self.send, self.arrive, self.here = send, arrive, here
+        self.remotes = self.locals = 0
+
+    def remote(self, src, dst, device, number=None):
+        if number is None:
+            number = self.remotes
+            self.remotes += 1
+        copy = pltpu.make_async_remote_copy(
+            src_ref=src, dst_ref=dst, send_sem=self.send.at[number], recv_sem=self.arrive.at[number],
+            device_id=device, device_id_type=MESH,
+        )
+        return copy, number
+
+    def local(self, src, dst):
+        number = self.locals
+        self.locals += 1
+        return pltpu.make_async_copy(src, dst, self.here.at[number])
+
+
+def fused_kernel(
+    dp,
+    states, cotangent, segments, qkv, out_w, up_w, down_w, pre, pack,
+    hidden, grads, pgrads, gup, gdown,
+    xb, xg, cot, lab_q, lab_k, qw, ow, uw, dw, pw, pk,
+    qs, kv, kvs, mg, lse, n1, r1, n2, r2, slopes,
+    mid, acc, act, mrecv, fsnd, fin, fout, fret, gsec, gfirst, gm, gms, gout,
+    keys, vals_t, vals, dk_acc, dv_acc, dq, dkv, dkv_send, dkv_recv, dxs, dxr, pacc, psib, pacross, psum, pdp,
+    send_sem, arrive_sem, here_sem,
+):
+    core, z, place = lax.axis_index("section"), lax.axis_index("dp"), lax.axis_index("tensor")
+    low, high = lax.rem(place, 2), place // 2
+    across = place + 1 - 2 * low
+    along = lax.rem(place + 2, 4)
+    sib_dev = {"section": 1 - core}
+    x_dev, y_dev = {"tensor": across}, {"tensor": along}
+    diag_dev = {"section": 1 - core, "tensor": across}
+
+    def dp_dev(step):
+        return {"dp": z + step - 2 * step * lax.rem(z // step, 2)}
+
+    dp_steps = []
+    while (1 << len(dp_steps)) < dp:
+        dp_steps.append(1 << len(dp_steps))
+    z_dev = dp_dev(1)
+    wires = Copies(send_sem, arrive_sem, here_sem)
+    pending = []
+
+    barrier = pltpu.get_barrier_semaphore()
+    greeted = [sib_dev, x_dev, y_dev, diag_dev] + [dp_dev(s) for s in dp_steps]
+    for device in greeted:
+        pl.semaphore_signal(barrier, inc=1, device_id=device, device_id_type=MESH)
+    pl.semaphore_wait(barrier, len(greeted))
+
+    half = lax.rem(z, 2) * (UNITS // 2)
+    other_half = UNITS // 2 - half
+
+    class Heads:
+        def __init__(self, layer):
+            self.layer = layer
+            items = [(qkv, qw, x_dev), (pre, pw, x_dev), (pack, pk, y_dev)]
+            self.here = [wires.local(src, dst.at[layer, 0]) for src, dst, _ in items]
+            self.over = [wires.remote(src, dst.at[layer, 1], dev)[0] for src, dst, dev in items]
+            self.first = [wires.remote(src, dst.at[layer, 0], sib_dev)[0] for src, dst, _ in items]
+            self.second = [wires.remote(dst.at[layer, 1], dst.at[layer, 1], sib_dev)[0] for _, dst, _ in items]
+
+        def start(self):
+            @pl.when(core == self.layer)
+            def _():
+                for c in self.over + self.here + self.first:
+                    c.start()
+
+        def forward(self):
+            @pl.when(core == self.layer)
+            def _():
+                for arriving, onward in zip(self.over, self.second, strict=True):
+                    arriving.wait_recv()
+                    onward.start()
+
+        def need(self):
+            @pl.when(core == self.layer)
+            def _():
+                for c in self.here:
+                    c.wait()
+
+            @pl.when(core != self.layer)
+            def _():
+                for c in self.first + self.second:
+                    c.wait_recv()
+
+        def finish(self):
+            @pl.when(core == self.layer)
+            def _():
+                for c in self.over + self.first + self.second:
+                    c.wait_send()
+
+    class Outs:
+        def __init__(self, layer):
+            self.layer = layer
+            self.here = wires.local(out_w, ow.at[layer, 0])
+            self.over = wires.remote(out_w, ow.at[layer, 1], x_dev)[0]
+            self.beside = wires.remote(out_w, ow.at[layer, 2], y_dev)[0]
+            self.third = wires.remote(ow.at[layer, 1], ow.at[layer, 3], y_dev)[0]
+            self.first = wires.remote(out_w, ow.at[layer, 0], sib_dev)[0]
+            self.rest = [wires.remote(ow.at[layer, i], ow.at[layer, i], sib_dev)[0] for i in (1, 2, 3)]
+
+        def start(self):
+            @pl.when(core == self.layer)
+            def _():
+                for c in (self.over, self.beside, self.here, self.first):
+                    c.start()
+
+        def forward(self):
+            @pl.when(core == self.layer)
+            def _():
+                self.over.wait_recv()
+                self.third.start()
+                self.rest[0].start()
+
+        def forward_last(self):
+            @pl.when(core == self.layer)
+            def _():
+                self.beside.wait_recv()
+                self.rest[1].start()
+                self.third.wait_recv()
+                self.rest[2].start()
+
+        def need(self):
+            @pl.when(core == self.layer)
+            def _():
+                self.here.wait()
+
+            @pl.when(core != self.layer)
+            def _():
+                for c in [self.first] + self.rest:
+                    c.wait_recv()
+
+        def finish(self):
+            @pl.when(core == self.layer)
+            def _():
+                for c in [self.over, self.beside, self.third, self.first] + self.rest:
+                    c.wait_send()
+
+    class Units:
+        def __init__(self, layer):
+            self.layer = layer
+            mine, theirs = pl.ds(half, UNITS // 2), pl.ds(other_half, UNITS // 2)
+            pairs = [(up_w, gup), (down_w, gdown)]
+            self.here = [wires.local(src, dst.at[layer, 0]) for src, dst in pairs]
+            self.first = [wires.remote(src, dst.at[layer, 0], sib_dev)[0] for src, dst in pairs]
+            self.over = [wires.remote(src.at[mine], dst.at[layer, 1, mine], y_dev)[0] for src, dst in pairs]
+            self.dp = [wires.remote(dst.at[layer, 1, mine], dst.at[layer, 1, mine], z_dev) for _, dst in pairs]
+            self.dp_in = [
+                wires.remote(dst.at[layer, 1, theirs], dst.at[layer, 1, theirs], z_dev, number)[0]
+                for (_, dst), (_, number) in zip(pairs, self.dp, strict=True)
+            ]
+            self.dp = [c for c, _ in self.dp]
+            self.rest = [wires.remote(dst.at[layer, 1, mine], dst.at[layer, 1, mine], sib_dev)[0] for _, dst in pairs]
+            self.last = [wires.remote(dst.at[layer, 1, theirs], dst.at[layer, 1, theirs], sib_dev)[0] for _, dst in pairs]
+
+        def start(self):
+            @pl.when(core == self.layer)
+            def _():
+                for c in self.over + self.here + self.first:
+                    c.start()
+
+        def forward(self, index):
+            @pl.when(core == self.layer)
+            def _():
+                self.over[index].wait_recv()
+                self.dp[index].start()
+                self.rest[index].start()
+
+        def forward_last(self, index):
+            @pl.when(core == self.layer)
+            def _():
+                self.dp_in[index].wait_recv()
+                self.last[index].start()
+
+        def need(self):
+            @pl.when(core == self.layer)
+            def _():
+                for c in self.here:
+                    c.wait()
+
+            @pl.when(core != self.layer)
+            def _():
+                for c in self.first + self.rest + self.last:
+                    c.wait_recv()
+
+        def finish(self):
+            @pl.when(core == self.layer)
+            def _():
+                for c in self.first + self.over + self.dp + self.rest + self.last:
+                    c.wait_send()
+
+    heads = [Heads(0), Heads(1)]
+    outs = [Outs(0), Outs(1)]
+    units = [Units(0), Units(1)]
+    loads = {}
+
+    def load_units(layer, when):
+        copies = [wires.local(gup.at[layer], uw), wires.local(gdown.at[layer], dw)]
+        for c in copies:
+            c.start()
+        loads[layer, when] = copies
+
+    def wait_units(layer, when):
+        for c in loads[layer, when]:
+            c.wait()
+
+    class Tokens:
+        def __init__(self, source, dest):
+            self.near = wires.local(source.at[low], dest)
+            self.far = wires.remote(source.at[1 - low], dest, x_dev)[0]
+
+        def start(self):
+            @pl.when(core == 0)
+            def _():
+                self.near.start()
+
+            @pl.when(core == 1)
+            def _():
+                self.far.start()
+
+        def wait(self):
+            @pl.when(core == 0)
+            def _():
+                self.near.wait()
+
+            @pl.when(core == 1)
+            def _():
+                self.far.wait_recv()
+
+        def finish(self):
+            @pl.when(core == 1)
+            def _():
+                self.far.wait_send()
+
+    tokens = Tokens(states, xb.at[0])
+    ends = Tokens(cotangent, cot)
+
+    tokens.start()
+    heads[0].start()
+    tokens.wait()
+
+    def chunk_rows(step):
+        return pl.ds(step * CHUNK, CHUNK)
+
+    def send_chunk(src, dst, device):
+        copy, _ = wires.remote(src, dst, device)
+        copy.start()
+        return copy
+
+    gathers = {}
+
+    def gather_x(layer, step):
+        gathers[layer, step] = send_chunk(
+            xb.at[layer, chunk_rows(step)], xg.at[chunk_rows(step)], y_dev
+        )
+
+    for step in range(STEPS):
+        gather_x(0, step)
+    units[0].start()
+    outs[0].start()
+
+    parity = low + core - 2 * low * core
+    row = segments[pl.ds(low, 1), :]
+    last = row[:, LEN - 1 :]
+
+    def block_labels(block):
+        ids = last - segments[pl.ds(low, 1), pl.ds(pl.multiple_of(block * ROWS, ROWS), ROWS)]
+        numbers = lax.broadcasted_iota(jnp.int32, (LABELS, ROWS), 0)
+        same = jnp.where(numbers == ids, 1.0, 0.0)
+        return same.T, jnp.where(numbers <= 2 * SPAN, HIDDEN * (1.0 - same), 0.0).T
+
+    for index, (h, p) in enumerate(((high, parity), (1 - high, parity), (high, 1 - parity), (1 - high, 1 - parity))):
+        same, differ = block_labels(2 * h + p)
+        if index < 2:
+            lab_q[pl.ds(index * ROWS, ROWS), :] = same.astype(BF16)
+        lab_k[pl.ds(index * ROWS, ROWS), :] = differ.astype(BF16)
+
+    def project(layer, source, start, size):
+        for slot in range(2):
+            columns = slice(slot * QUARTER, (slot + 1) * QUARTER)
+            rows = pl.ds(start, size)
+            qs[layer, rows, columns] = dot(source, qw[layer, slot, 0]).astype(BF16)
+            kv[layer, rows, columns] = dot(source, qw[layer, slot, 1]).astype(BF16)
+            kv[layer, rows, slice(CORE + columns.start, CORE + columns.stop)] = dot(
+                source, qw[layer, slot, 2]
+            ).astype(BF16)
+
+    def lanes(index, base=0):
+        return pl.ds(pl.multiple_of(base + index * PAIR, PAIR), PAIR)
+
+    def fill(layer, p):
+        pre_lanes = pl.ds(pl.multiple_of(lax.rem(p, 2) * PAIR, PAIR), PAIR)
+        keys[:CORE, :PAIR] = kv[layer, :, lanes(p)]
+        keys[CORE : 2 * CORE, :PAIR] = kvs[layer, :, lanes(p)]
+        keys[2 * CORE :, :PAIR] = pw[layer, p // 2, 0, :, pre_lanes]
+        return kv[layer, :, lanes(p, CORE)], kvs[layer, :, lanes(p, CORE)], pw[layer, p // 2, 1, :, pre_lanes]
+
+    keys[: 2 * CORE, PAIR:] = lab_k[...]
+    keys[2 * CORE :, PAIR:] = jnp.zeros((PREFIX, LABELS), BF16)
+
+    def attend_rows(layer, start):
+        rows = pl.ds(start, ROWS)
+
+        def body(p, _):
+            vo, vs, vp = fill(layer, p)
+            vals_t[:, :CORE] = vo.T
+            vals_t[:, CORE : 2 * CORE] = vs.T
+            vals_t[:, 2 * CORE :] = vp.T
+            query = qs[layer, rows, lanes(p)] * 0.125
+            label = lab_q[rows, :]
+            results = []
+            for head in range(2):
+                mine = jnp.where(head_lanes(ROWS, head), query, 0)
+                scores = dot_t(keys[...], jnp.concatenate([mine, label], 1))
+                peak = jnp.max(scores, axis=0, keepdims=True)
+                weights = jnp.exp(scores - peak)
+                total = jnp.sum(weights, axis=0, keepdims=True)
+                merged = dot(vals_t[head * HEAD : (head + 1) * HEAD, :], weights.astype(BF16))
+                results.append(merged / total)
+                lse[layer, p, head : head + 1, rows] = peak + jnp.log(total)
+            mg[layer, rows, lanes(p)] = jnp.concatenate(results, 0).T.astype(BF16)
+            return 0
+
+        lax.fori_loop(0, PAIRS, body, 0)
+
+    def attend_rows_back(layer, start, fresh):
+        rows = pl.ds(start, ROWS)
+
+        def body(p, _):
+            vo, vs, vp = fill(layer, p)
+            vals[:CORE, :] = vo
+            vals[CORE : 2 * CORE, :] = vs
+            vals[2 * CORE :, :] = vp
+            vals_t[:, :CORE] = keys[:CORE, :PAIR].T
+            vals_t[:, CORE : 2 * CORE] = keys[CORE : 2 * CORE, :PAIR].T
+            vals_t[:, 2 * CORE :] = keys[2 * CORE :, :PAIR].T
+            query = qs[layer, rows, lanes(p)] * 0.125
+            label = lab_q[rows, :]
+            grad_part = gm[rows, lanes(p)]
+            product = (grad_part.astype(F32) * mg[layer, rows, lanes(p)].astype(F32)).T
+            queries, grad_list, weights_all, scores_all, results = [], [], [], [], []
+            for head in range(2):
+                span = slice(head * HEAD, (head + 1) * HEAD)
+                mine = jnp.where(head_lanes(ROWS, head), query, 0)
+                mine_grad = jnp.where(head_lanes(ROWS, head), grad_part, 0)
+                scores = dot_t(keys[...], jnp.concatenate([mine, label], 1))
+                weights = jnp.exp(scores - lse[layer, p, head : head + 1, rows])
+                delta = jnp.sum(product[span], axis=0, keepdims=True)
+                grad_scores = (weights * (dot_t(vals[...], mine_grad) - delta)).astype(BF16)
+                results.append(dot(vals_t[span, :], grad_scores))
+                queries.append(mine)
+                grad_list.append(mine_grad)
+                weights_all.append(weights.astype(BF16))
+                scores_all.append(grad_scores)
+            dq[rows, lanes(p)] = (jnp.concatenate(results, 0).T * 0.125).astype(BF16)
+            dv_part = dot(jnp.concatenate(weights_all, 1), jnp.concatenate(grad_list, 0))
+            dk_part = dot(jnp.concatenate(scores_all, 1), jnp.concatenate(queries, 0))
+            if fresh:
+                dv_acc[:, lanes(p)] = dv_part
+                dk_acc[:, lanes(p)] = dk_part
+            else:
+                dv_acc[:, lanes(p)] += dv_part
+                dk_acc[:, lanes(p)] += dk_part
+            return 0
+
+        lax.fori_loop(0, PAIRS, body, 0)
+
+    def vector(layer, index):
+        return pk[layer, 0, index : index + 1, :]
+
+    def keep_norm(store, scales, layer, rows, normed, scale):
+        store[layer, rows, :] = normed.astype(BF16)
+        scales[layer, rows, :] = jnp.broadcast_to(scale, (CHUNK, PAIR))
+
+    def forward_attention(layer):
+        if layer == 0:
+            heads[0].forward()
+        heads[layer].need()
+        project(layer, xb[layer], 0, ROWS)
+        sent = [send_chunk(kv.at[layer, :ROWS], kvs.at[layer, :ROWS], sib_dev)]
+        for step in range(STEPS):
+            gathers[layer, step].wait_recv()
+            project(layer, xg[chunk_rows(step), :], ROWS + step * CHUNK, CHUNK)
+        sent.append(send_chunk(kv.at[layer, ROWS:], kvs.at[layer, ROWS:], sib_dev))
+        if layer == 0:
+            heads[1].start()
+            outs[0].forward()
+            units[0].forward(0)
+        for c in sent:
+            c.wait_recv()
+        attend_rows(layer, ROWS)
+        swap = send_chunk(mg.at[layer, ROWS:], mrecv, y_dev)
+        if layer == 0:
+            outs[0].forward_last()
+            units[0].forward(1)
+            units[0].forward_last(0)
+        else:
+            units[1].forward(1)
+            units[1].forward_last(0)
+        attend_rows(layer, 0)
+        if layer == 0:
+            outs[1].start()
+            ends.start()
+            units[0].forward_last(1)
+            units[0].need()
+            load_units(0, 0)
+        else:
+            units[1].forward_last(1)
+            units[1].need()
+            load_units(1, 0)
+        outs[layer].need()
+        swap.wait_recv()
+        copies = []
+        for step in range(STEPS):
+            rows = chunk_rows(step)
+            parts = [mg[layer, rows, :QUARTER], mg[layer, rows, QUARTER:], mrecv[rows, :QUARTER], mrecv[rows, QUARTER:]]
+            total = xb[layer, rows, :].astype(F32) + vector(layer, 3)
+            for i, part in enumerate(parts):
+                total = total + dot(part, ow[layer, i])
+            normed, scale = norm_chunk(total)
+            keep_norm(n1, r1, layer, rows, normed, scale)
+            middle = normed * vector(layer, 1) + vector(layer, 4)
+            mid[rows, :] = middle
+            fsnd[rows, :] = middle.astype(BF16)
+            copies.append(send_chunk(fsnd.at[rows], fin.at[rows], x_dev))
+        for c in sent + [swap] + [gathers[layer, s] for s in range(STEPS)]:
+            c.wait_send()
+        return copies
+
+    def feed_rows(layer, source, start, size):
+        def up_tile(j, _):
+            slot, columns = j // 4, pl.ds(pl.multiple_of(lax.rem(j, 4) * TILE, TILE), TILE)
+            wide = pl.ds(pl.multiple_of(j * TILE, TILE), TILE)
+            u = dot(source[...], uw[slot, :, columns]) + pk[layer, slot, 0:1, columns]
+            act[:size, wide], slopes[layer, pl.ds(start, size), wide] = gelu_both(u)
+            return 0
+
+        lax.fori_loop(0, 2 * UNITS // TILE, up_tile, 0)
+
+    def feed_rows_back(layer, source, start, size):
+        def tile(j, _):
+            slot, units_at = j // 4, pl.ds(pl.multiple_of(lax.rem(j, 4) * TILE, TILE), TILE)
+            wide = pl.ds(pl.multiple_of(j * TILE, TILE), TILE)
+            u = dot_t(source[...], dw[slot, units_at, :]) * slopes[layer, pl.ds(start, size), wide].astype(F32)
+            act[:size, wide] = u.astype(BF16)
+            return 0
+
+        lax.fori_loop(0, 2 * UNITS // TILE, tile, 0)
+
+    def feed_out(store, size, back):
+        def tile(j, _):
+            columns = pl.ds(pl.multiple_of(j * TILE, TILE), TILE)
+            if back:
+                u = dot_t(act[:size, :UNITS], uw[0, columns, :]) + dot_t(act[:size, UNITS:], uw[1, columns, :])
+            else:
+                u = dot(act[:size, :UNITS], dw[0, :, columns]) + dot(act[:size, UNITS:], dw[1, :, columns])
+            store[:, columns] = u.astype(store.dtype)
+            return 0
+
+        lax.fori_loop(0, D // TILE, tile, 0)
+
+    def feed(layer, copies, back, finish):
+        rows_fn = feed_rows_back if back else feed_rows
+        rows_fn(layer, fsnd, 0, ROWS)
+        feed_out(acc, ROWS, back)
+        returned = []
+        for step in range(STEPS):
+            rows = chunk_rows(step)
+            copies[step].wait_recv()
+            rows_fn(layer, fin.at[rows], ROWS + step * CHUNK, CHUNK)
+            feed_out(fout.at[rows], CHUNK, back)
+            returned.append(send_chunk(fout.at[rows], fret.at[rows], x_dev))
+        for step in range(STEPS):
+            returned[step].wait_recv()
+            finish(step, chunk_rows(step), acc[chunk_rows(step), :] + fret[chunk_rows(step), :].astype(F32))
+        for c in copies + returned:
+            c.wait_send()
+
+    deliveries = []
+
+    def deliver(layer, source, dest, step):
+        rows = chunk_rows(step)
+        far, number = wires.remote(source.at[rows], dest.at[low, rows], {"section": layer, "tensor": across})
+        far_in, _ = wires.remote(source.at[rows], dest.at[1 - low, rows], {"section": layer, "tensor": across}, number)
+        if layer == 0:
+            near = wires.local(source.at[rows], dest.at[low, rows])
+        else:
+            near, _ = wires.remote(source.at[rows], dest.at[low, rows], sib_dev)
+
+        @pl.when(core == 0)
+        def _():
+            near.start()
+
+        @pl.when(core == 1)
+        def _():
+            far.start()
+
+        def sent():
+            @pl.when(core == 0)
+            def _():
+                near.wait() if layer == 0 else near.wait_send()
+
+            @pl.when(core == 1)
+            def _():
+                far.wait_send()
+
+        def arrived():
+            @pl.when(core == layer)
+            def _():
+                far_in.wait_recv()
+                if layer == 1:
+                    near.wait_recv()
+
+        deliveries.append(arrived)
+        return sent
+
+    def start_back(layer, step, rows, grad):
+        normed, scale = n2[layer, rows, :].astype(F32), r2[layer, rows, :1]
+        value = norm_back(grad, vector(layer, 2), normed, scale)
+        gsec[rows, :] = value
+        fsnd[rows, :] = value.astype(BF16)
+        return send_chunk(fsnd.at[rows], fin.at[rows], x_dev)
+
+    unsent = []
+    back_copies = []
+
+    def forward_finish(layer):
+        def finish(step, rows, branch):
+            normed, scale = norm_chunk(mid[rows, :] + branch + vector(layer, 5))
+            keep_norm(n2, r2, layer, rows, normed, scale)
+            xb[layer + 1, rows, :] = (normed * vector(layer, 2) + vector(layer, 6)).astype(BF16)
+            if layer == 0:
+                gather_x(1, step)
+            unsent.append(deliver(layer, xb.at[layer + 1], hidden, step))
+
+        return finish
+
+    copies = forward_attention(0)
+    wait_units(0, 0)
+    heads[1].forward()
+    units[1].start()
+    outs[1].forward()
+    feed(0, copies, False, forward_finish(0))
+    outs[1].forward_last()
+    units[1].forward(0)
+    copies = forward_attention(1)
+    wait_units(1, 0)
+    feed(1, copies, False, forward_finish(1))
+
+    ends.wait()
+    for step in range(STEPS):
+        back_copies.append(start_back(1, step, chunk_rows(step), cot[chunk_rows(step), :].astype(F32)))
+
+    grad_sent = []
+
+    def backward(layer, copies):
+        swaps = []
+
+        def finish(step, rows, term):
+            middle = gsec[rows, :] + term
+            first = norm_back(middle, vector(layer, 1), n1[layer, rows, :].astype(F32), r1[layer, rows, :1])
+            gfirst[rows, :] = first
+            low_first = first.astype(BF16)
+            for i in range(4):
+                part = dot_t(low_first, ow[layer, i]).astype(BF16)
+                columns = slice((i % 2) * QUARTER, (i % 2 + 1) * QUARTER)
+                if i < 2:
+                    gm[rows, columns] = part
+                else:
+                    gms[rows, columns] = part
+            swaps.append(send_chunk(gms.at[rows], gm.at[pl.ds(ROWS + step * CHUNK, CHUNK)], y_dev))
+
+        feed(layer, copies, True, finish)
+        if layer == 1:
+            load_units(0, 1)
+        attend_rows_back(layer, 0, True)
+        for c in swaps:
+            c.wait_recv()
+        attend_rows_back(layer, ROWS, False)
+        dkv_send[:, :CORE] = dk_acc[CORE : 2 * CORE, :].astype(BF16)
+        dkv_send[:, CORE:] = dv_acc[CORE : 2 * CORE, :].astype(BF16)
+        given = send_chunk(dkv_send, dkv_recv.at[layer], sib_dev)
+        pacc[layer, 0] = dk_acc[2 * CORE :, :]
+        pacc[layer, 1] = dv_acc[2 * CORE :, :]
+        if layer == 0:
+            total = prefix_start()
+        given.wait_recv()
+        dkv[:, :CORE] = (dk_acc[:CORE, :] + dkv_recv[layer, :, :CORE].astype(F32)).astype(BF16)
+        dkv[:, CORE:] = (dv_acc[:CORE, :] + dkv_recv[layer, :, CORE:].astype(F32)).astype(BF16)
+
+        def input_term(store, start, size):
+            rows = pl.ds(start, size)
+
+            def tile(j, _):
+                features = pl.ds(pl.multiple_of(j * TILE, TILE), TILE)
+                total = None
+                for slot in range(2):
+                    columns = slice(slot * QUARTER, (slot + 1) * QUARTER)
+                    shifted = slice(CORE + slot * QUARTER, CORE + (slot + 1) * QUARTER)
+                    for part, source in enumerate((dq[rows, columns], dkv[rows, columns], dkv[rows, shifted])):
+                        term = dot_t(source, qw[layer, slot, part, features, :])
+                        total = term if total is None else total + term
+                store[:, features] = total.astype(store.dtype)
+                return 0
+
+            lax.fori_loop(0, D // TILE, tile, 0)
+
+        returned = []
+        for step in range(STEPS):
+            input_term(dxs.at[chunk_rows(step)], ROWS + step * CHUNK, CHUNK)
+            returned.append(send_chunk(dxs.at[chunk_rows(step)], dxr.at[chunk_rows(step)], y_dev))
+        if layer == 0:
+            total.stage()
+        input_term(acc, 0, ROWS)
+        if layer == 1:
+            wait_units(0, 1)
+        else:
+            total.stage()
+        for sent in grad_sent:
+            sent()
+        grad_sent.clear()
+        onward = []
+        for step in range(STEPS):
+            rows = chunk_rows(step)
+            returned[step].wait_recv()
+            value = gfirst[rows, :] + (acc[rows, :] + dxr[rows, :].astype(F32))
+            gout[rows, :] = value
+            grad_sent.append(deliver(layer, gout, grads, step))
+            if layer == 1:
+                onward.append(start_back(0, step, rows, value.astype(BF16).astype(F32)))
+            else:
+                total.stage()
+        for c in swaps + [given] + returned:
+            c.wait_send()
+        return onward
+
+    class prefix_start:
+        def __init__(self):
+            self.sib = send_chunk(pacc.at[1 - core], psib, sib_dev)
+            self.sent = [self.sib]
+            self.at = 0
+
+        def stage(self):
+            if self.at == 0:
+                self.sib.wait_recv()
+                total = pacc[core] + psib[...]
+                psum[0] = total[:, :, :QUARTER]
+                pacross[0] = total[:, :, QUARTER:]
+                self.next = send_chunk(pacross.at[0], pacross.at[1], x_dev)
+                self.sent.append(self.next)
+            elif self.at <= len(dp_steps) + 1:
+                self.next.wait_recv()
+                arrived = pacross[1] if self.at == 1 else pdp[self.at - 2]
+                psum[self.at] = psum[self.at - 1] + arrived
+                if self.at <= len(dp_steps):
+                    step = self.at - 1
+                    self.next = send_chunk(psum.at[self.at], pdp.at[step], dp_dev(dp_steps[step]))
+                    self.sent.append(self.next)
+                else:
+                    self.done = wires.local(psum.at[self.at], pgrads)
+                    self.done.start()
+            self.at += 1
+
+        def finish(self):
+            while self.at <= len(dp_steps) + 1:
+                self.stage()
+            for c in self.sent:
+                c.wait_send()
+            self.done.wait()
+
+    holder = []
+    start_class = prefix_start
+
+    def prefix_start():
+        holder.append(start_class())
+        return holder[0]
+
+    back_copies = backward(1, back_copies)
+    backward(0, back_copies)
+    holder[0].finish()
+    for sent in unsent + grad_sent:
+        sent()
+    for arrived in deliveries:
+        arrived()
+    tokens.finish()
+    ends.finish()
+    for layer in range(2):
+        heads[layer].finish()
+        outs[layer].finish()
+        units[layer].finish()
+
+
+def fused(dp, states, cotangent, segments, qkv, out_w, up_w, down_w, pre, pack):
+    shape = jax.ShapeDtypeStruct
+    steps = dp.bit_length() - 1
+    vmem = pltpu.VMEM
+    scratch = [
+        vmem((3, ROWS, D), BF16),
+        vmem((ROWS, D), BF16),
+        vmem((ROWS, D), BF16),
+        vmem((CORE, LABELS), BF16), vmem((2 * CORE, LABELS), BF16),
+        vmem((2, 2, 3, D, QUARTER), BF16),
+        vmem((2, 4, QUARTER, D), BF16),
+        vmem((2, D, UNITS), BF16), vmem((2, UNITS, D), BF16),
+        vmem((2, 2, 2, PREFIX, QUARTER), BF16),
+        vmem((2, 2, 8, D), F32),
+        vmem((2, CORE, CORE), BF16), vmem((2, CORE, 2 * CORE), BF16), vmem((2, CORE, 2 * CORE), BF16),
+        vmem((2, CORE, CORE), BF16), vmem((2, PAIRS, 8, CORE), F32),
+        vmem((2, ROWS, D), BF16), vmem((2, ROWS, PAIR), F32),
+        vmem((2, ROWS, D), BF16), vmem((2, ROWS, PAIR), F32),
+        vmem((2, CORE, 2 * UNITS), BF16),
+        vmem((ROWS, D), F32), vmem((ROWS, D), F32), vmem((ROWS, 2 * UNITS), BF16),
+        vmem((ROWS, CORE), BF16),
+        vmem((ROWS, D), BF16), vmem((ROWS, D), BF16), vmem((ROWS, D), BF16), vmem((ROWS, D), BF16),
+        vmem((ROWS, D), F32), vmem((ROWS, D), F32),
+        vmem((CORE, CORE), BF16), vmem((ROWS, CORE), BF16), vmem((ROWS, D), F32),
+        vmem((KEYS, PAIR + LABELS), BF16), vmem((PAIR, KEYS), BF16), vmem((KEYS, PAIR), BF16),
+        vmem((KEYS, CORE), F32), vmem((KEYS, CORE), F32),
+        vmem((CORE, CORE), BF16), vmem((CORE, 2 * CORE), BF16), vmem((CORE, 2 * CORE), BF16),
+        vmem((2, CORE, 2 * CORE), BF16),
+        vmem((ROWS, D), BF16), vmem((ROWS, D), BF16),
+        vmem((2, 2, PREFIX, CORE), F32), vmem((2, PREFIX, CORE), F32),
+        vmem((2, 2, PREFIX, QUARTER), F32), vmem((steps + 2, 2, PREFIX, QUARTER), F32),
+        vmem((max(steps, 1), 2, PREFIX, QUARTER), F32),
+        pltpu.SemaphoreType.DMA((SEMS,)), pltpu.SemaphoreType.DMA((SEMS,)), pltpu.SemaphoreType.DMA((SEMS,)),
+    ]
+    anywhere = pl.BlockSpec(memory_space=pl.ANY)
+    result = pl.pallas_call(
+        functools.partial(fused_kernel, dp),
+        out_shape=[
+            shape((2, ROWS, D), BF16), shape((2, ROWS, D), F32), shape((2, PREFIX, QUARTER), F32),
+            shape((2, 2, D, UNITS), BF16), shape((2, 2, UNITS, D), BF16),
+        ],
+        in_specs=[anywhere, anywhere, pl.BlockSpec(memory_space=pltpu.VMEM)] + [anywhere] * 6,
+        out_specs=[anywhere] * 5,
+        scratch_shapes=scratch,
+        compiler_params=pltpu.CompilerParams(
+            collective_id=0, has_side_effects=True, vmem_limit_bytes=63 << 20
+        ),
+        name="layers",
+    )(states, cotangent, segments, qkv, out_w, up_w, down_w, pre, pack)
+    return result[:3]
+
+
 class Links:
     def __init__(self):
         self.core = lax.axis_index("section")
@@ -310,7 +1089,7 @@
     return a
 
 
-def local(
+def plain(
     states, segment_ids, cotangent, qkv_weight, out_weight, up_weight, up_bias, down_weight,
     norm_gain, shift_vec, prefix,
 ):
@@ -384,6 +1163,23 @@
     return hidden_out[None], input_grads[None], prefix_grads[None]
 
 
+def whole_kernel(
+    states, segment_ids, cotangent, qkv_weight, out_weight, up_weight, up_bias, down_weight,
+    norm_gain, shift_vec, prefix,
+):
+    pack = jnp.concatenate([up_bias, norm_gain[0], shift_vec[0], jnp.zeros_like(up_bias)], 0).astype(F32)
+    results = fused(
+        lax.axis_size("dp"), states, cotangent, segment_ids, jnp.transpose(qkv_weight[0], (1, 0, 2)),
+        out_weight[0], up_weight[0], down_weight[0], prefix[0], pack,
+    )
+    return tuple(r[None] for r in results)
+
+
+def fits(mesh):
+    dp = mesh.shape["dp"]
+    return mesh.shape["tensor"] == 4 and dp > 1 and dp & (dp - 1) == 0
+
+
 def solution(mesh):
     placed = (
         P(None, ("dp", "tensor"), None),
@@ -399,7 +1195,7 @@
         P("section", None, None, "tensor"),
     )
     return jax.shard_map(
-        local,
+        whole_kernel if fits(mesh) else plain,
         mesh=mesh,
         in_specs=placed,
         out_specs=(

time: 499 us -> 365 us (0.73); the launches traced: 489 us -> 364 us
  Pallas kernels: 54.3 us -> 358 us
  waiting for transfers between devices: 229 us -> 0 us
  starting transfers between devices: 96 us -> 0 us
  matrix products: 59.8 us -> 0 us
  other arithmetic: 33.4 us -> 1.41 us
  local copies, waits for them, and re-layouts: 13 us -> 4.47 us
    pallas_call x4 -> x1, Pallas kernels: 54.3 us -> 358 us  [fused(): pl.pallas_call(functools.partial(fused_kernel, dp), out_shape=[shape((2,...]
    ppermute x69 -> x0, waiting for transfers between devices: 229 us -> none  [the longest x16 162 us: from_ahead(): return lax.ppermute(a, 'tensor', pairs)]
    ppermute x69 -> x0, starting transfers between devices: 96 us -> none  [the longest x32 53.1 us: sibling(): return lax.ppermute(a, 'section', pairs)]
    dot_general x28 -> x0, matrix products: 59.8 us -> none  [the longest x12 43.3 us: dot_t(): lax.dot_general(a, b, (((1,), (1,)), ((), ())), preferred_element_type=F32)]
    select_n x20 -> x0, other arithmetic: 13.8 us -> none  [the longest x6 10.6 us: spread_weights(): jnp.where(here, a, sib_a)]
    convert_element_type x16 -> x1, other arithmetic: 9.4 us -> 1.41 us  [whole_kernel(): jnp.concatenate([up_bias, norm_gain[0], shift_vec[0], jnp.zeros_like(up_b...]
  transfers between devices with their start and end apart: 69 -> 0, of which waited for: 29 -> 0; matrix products, arithmetic and copies ran while one was open for 10% -> 0% of each run, Pallas kernels for 5% -> 0%
where the time goes in v2:
time: 365 us; the launch traced here: 364 us
  Pallas kernels  358 us (98%)
  local copies, waits for them, and re-layouts  4.47 us (1%)
    pallas_call x1, Pallas kernels, fused(): pl.pallas_call(functools.partial(fused_kernel, dp), out_shape=[shape((2,...  358 us

profile of v2, /device:TPU:0, one launch (start us, length us, event | category | flops | bytes accessed | tf_op | source)
XLA Modules:
  0.0 364.4 jit_solution(8755624290391674239)
XLA Ops:
  0.6 0.1 pad.3.clone
  0.7 1.4 maximum_convert_fusion.pack
  2.1 357.8 %layers.1 = (bf16[2,256,1024]{2,1,0:T(8,128)(2,1)}, f32[2,256,1024]{2,1,0:T(8,128)}, f32[2,64,256]{2,1,0:T(8,128)}, bf16[2,2,1024,1024]{3,2,1,0:T(8,128)(2,1)}, bf16[2,2,1024,1024]{3,2,1,0:T(8,128)(2,1)}) custom-call(bf16[2,256,1024]{2,1,0:T(8,128)(2,1)} %states.1, bf16[2,256,1024]{2,1,0:T(8,128)(2,1)} %cotangent.1, s32[2,1024]{1,0:T(2,128)} %segments.1, ...), custom_call_target="tpu_custom_call" | custom-call | tf_op jit(solution)/shard_map/layers/pallas_call | solution.py:968
  360.0 0.0 copy-start
  360.0 2.4 copy.17
  362.4 0.0 copy-done
  362.4 0.0 copy-start.1
  362.4 1.3 copy.18
  363.7 0.0 copy-done.1
  363.7 0.7 copy.19
Async XLA Ops:
  360.0 2.4 copy-start
  362.4 1.3 copy-start.1

commit v3 on v2

--- a/solution.py
+++ b/solution.py
@@ -213,7 +213,7 @@
 TILE = 256
 PAIRS = 4
 KEYS = 2 * CORE + PREFIX
-SEMS = 128
+SEMS = 192
 
 
 def gelu_both(u):
@@ -247,9 +247,10 @@
         )
         return copy, number
 
-    def local(self, src, dst):
-        number = self.locals
-        self.locals += 1
+    def local(self, src, dst, number=None):
+        if number is None:
+            number = self.locals
+            self.locals += 1
         return pltpu.make_async_copy(src, dst, self.here.at[number])
 
 
@@ -287,158 +288,189 @@
         pl.semaphore_signal(barrier, inc=1, device_id=device, device_id_type=MESH)
     pl.semaphore_wait(barrier, len(greeted))
 
-    half = lax.rem(z, 2) * (UNITS // 2)
-    other_half = UNITS // 2 - half
-
-    class Heads:
-        def __init__(self, layer):
+    class Own:
+        def __init__(self, layer, src, dst):
             self.layer = layer
-            items = [(qkv, qw, x_dev), (pre, pw, x_dev), (pack, pk, y_dev)]
-            self.here = [wires.local(src, dst.at[layer, 0]) for src, dst, _ in items]
-            self.over = [wires.remote(src, dst.at[layer, 1], dev)[0] for src, dst, dev in items]
-            self.first = [wires.remote(src, dst.at[layer, 0], sib_dev)[0] for src, dst, _ in items]
-            self.second = [wires.remote(dst.at[layer, 1], dst.at[layer, 1], sib_dev)[0] for _, dst, _ in items]
+            self.here = wires.local(src, dst)
+            self.first = wires.remote(src, dst, sib_dev)[0]
 
         def start(self):
             @pl.when(core == self.layer)
             def _():
-                for c in self.over + self.here + self.first:
-                    c.start()
+                self.here.start()
+                self.first.start()
+
+        def need(self):
+            @pl.when(core == self.layer)
+            def _():
+                self.here.wait()
+
+            @pl.when(core != self.layer)
+            def _():
+                self.first.wait_recv()
+
+        def finish(self):
+            @pl.when(core == self.layer)
+            def _():
+                self.first.wait_send()
+
+    class Away:
+        def __init__(self, layer, src, dst):
+            self.layer = layer
+            self.first = wires.remote(src, dst, sib_dev)[0]
+
+        def start(self):
+            @pl.when(core == self.layer)
+            def _():
+                self.first.start()
+
+        def need(self):
+            @pl.when(core != self.layer)
+            def _():
+                self.first.wait_recv()
+
+        def finish(self):
+            @pl.when(core == self.layer)
+            def _():
+                self.first.wait_send()
+
+    class Direct:
+        def __init__(self, layer, src, dst, dev):
+            self.layer = layer
+            self.over = wires.remote(src, dst, dev)[0]
+            self.rest = wires.remote(dst, dst, sib_dev)[0]
+
+        def start(self):
+            @pl.when(core == self.layer)
+            def _():
+                self.over.start()
 
         def forward(self):
             @pl.when(core == self.layer)
             def _():
-                for arriving, onward in zip(self.over, self.second, strict=True):
-                    arriving.wait_recv()
-                    onward.start()
+                self.over.wait_recv()
+                self.rest.start()
 
         def need(self):
-            @pl.when(core == self.layer)
-            def _():
-                for c in self.here:
-                    c.wait()
-
             @pl.when(core != self.layer)
             def _():
-                for c in self.first + self.second:
-                    c.wait_recv()
+                self.rest.wait_recv()
 
         def finish(self):
             @pl.when(core == self.layer)
             def _():
-                for c in self.over + self.first + self.second:
-                    c.wait_send()
-
-    class Outs:
-        def __init__(self, layer):
+                self.over.wait_send()
+                self.rest.wait_send()
+
+    class Shared:
+        def __init__(self, layer, src, dst, mine, theirs, dev):
             self.layer = layer
-            self.here = wires.local(out_w, ow.at[layer, 0])
-            self.over = wires.remote(out_w, ow.at[layer, 1], x_dev)[0]
-            self.beside = wires.remote(out_w, ow.at[layer, 2], y_dev)[0]
-            self.third = wires.remote(ow.at[layer, 1], ow.at[layer, 3], y_dev)[0]
-            self.first = wires.remote(out_w, ow.at[layer, 0], sib_dev)[0]
-            self.rest = [wires.remote(ow.at[layer, i], ow.at[layer, i], sib_dev)[0] for i in (1, 2, 3)]
+            self.over = wires.remote(src.at[mine], dst.at[mine], dev)[0]
+            self.dp, number = wires.remote(dst.at[mine], dst.at[mine], z_dev)
+            self.dp_in = wires.remote(dst.at[theirs], dst.at[theirs], z_dev, number)[0]
+            self.rest = wires.remote(dst.at[mine], dst.at[mine], sib_dev)[0]
+            self.last = wires.remote(dst.at[theirs], dst.at[theirs], sib_dev)[0]
 
         def start(self):
             @pl.when(core == self.layer)
             def _():
-                for c in (self.over, self.beside, self.here, self.first):
-                    c.start()
+                self.over.start()
 
         def forward(self):
             @pl.when(core == self.layer)
             def _():
                 self.over.wait_recv()
-                self.third.start()
-                self.rest[0].start()
+                self.dp.start()
+                self.rest.start()
 
         def forward_last(self):
             @pl.when(core == self.layer)
             def _():
-                self.beside.wait_recv()
-                self.rest[1].start()
-                self.third.wait_recv()
-                self.rest[2].start()
+                self.dp_in.wait_recv()
+                self.last.start()
 
         def need(self):
-            @pl.when(core == self.layer)
-            def _():
-                self.here.wait()
-
             @pl.when(core != self.layer)
             def _():
-                for c in [self.first] + self.rest:
-                    c.wait_recv()
+                self.rest.wait_recv()
+                self.last.wait_recv()
 
         def finish(self):
             @pl.when(core == self.layer)
             def _():
-                for c in [self.over, self.beside, self.third, self.first] + self.rest:
+                for c in (self.over, self.dp, self.rest, self.last):
                     c.wait_send()
 
-    class Units:
+    odd = lax.rem(z, 2)
+
+    def halves(size, pieces):
+        step = size // 2 // pieces
+        return [
+            tuple(pl.ds(pl.multiple_of(parity_z * (size // 2) + i * step, step), step) for parity_z in (odd, 1 - odd))
+            for i in range(pieces)
+        ]
+
+    class Layer:
         def __init__(self, layer):
-            self.layer = layer
-            mine, theirs = pl.ds(half, UNITS // 2), pl.ds(other_half, UNITS // 2)
-            pairs = [(up_w, gup), (down_w, gdown)]
-            self.here = [wires.local(src, dst.at[layer, 0]) for src, dst in pairs]
-            self.first = [wires.remote(src, dst.at[layer, 0], sib_dev)[0] for src, dst in pairs]
-            self.over = [wires.remote(src.at[mine], dst.at[layer, 1, mine], y_dev)[0] for src, dst in pairs]
-            self.dp = [wires.remote(dst.at[layer, 1, mine], dst.at[layer, 1, mine], z_dev) for _, dst in pairs]
-            self.dp_in = [
-                wires.remote(dst.at[layer, 1, theirs], dst.at[layer, 1, theirs], z_dev, number)[0]
-                for (_, dst), (_, number) in zip(pairs, self.dp, strict=True)
+            self.heads_own = Own(layer, qkv, qw.at[layer, 0])
+            self.small_own = [Own(layer, pre, pw.at[layer, 0]), Own(layer, pack, pk.at[layer, 0])]
+            self.out_own = Own(layer, out_w, ow.at[layer, 0])
+            self.units_own = [Away(layer, up_w, gup.at[layer, 0]), Away(layer, down_w, gdown.at[layer, 0])]
+            if layer == 0:
+                (mine, theirs), = halves(D, 1)
+                self.heads = [
+                    Shared(layer, qkv.at[i], qw.at[layer, 1, i], mine, theirs, x_dev) for i in range(3)
+                ]
+            else:
+                self.heads = [Direct(layer, qkv, qw.at[layer, 1], x_dev)]
+            self.small = [Direct(layer, pre, pw.at[layer, 1], x_dev), Direct(layer, pack, pk.at[layer, 1], y_dev)]
+            self.out_x = Direct(layer, out_w, ow.at[layer, 1], x_dev)
+            (mine, theirs), = halves(QUARTER, 1)
+            self.out_y = [
+                Shared(layer, out_w, ow.at[layer, 2], mine, theirs, y_dev),
+                Shared(layer, ow.at[layer, 1], ow.at[layer, 3], mine, theirs, y_dev),
             ]
-            self.dp = [c for c, _ in self.dp]
-            self.rest = [wires.remote(dst.at[layer, 1, mine], dst.at[layer, 1, mine], sib_dev)[0] for _, dst in pairs]
-            self.last = [wires.remote(dst.at[layer, 1, theirs], dst.at[layer, 1, theirs], sib_dev)[0] for _, dst in pairs]
-
-        def start(self):
-            @pl.when(core == self.layer)
-            def _():
-                for c in self.over + self.here + self.first:
-                    c.start()
-
-        def forward(self, index):
-            @pl.when(core == self.layer)
-            def _():
-                self.over[index].wait_recv()
-                self.dp[index].start()
-                self.rest[index].start()
-
-        def forward_last(self, index):
-            @pl.when(core == self.layer)
-            def _():
-                self.dp_in[index].wait_recv()
-                self.last[index].start()
-
-        def need(self):
-            @pl.when(core == self.layer)
-            def _():
-                for c in self.here:
-                    c.wait()
-
-            @pl.when(core != self.layer)
-            def _():
-                for c in self.first + self.rest + self.last:
-                    c.wait_recv()
-
-        def finish(self):
-            @pl.when(core == self.layer)
-            def _():
-                for c in self.first + self.over + self.dp + self.rest + self.last:
-                    c.wait_send()
-
-    heads = [Heads(0), Heads(1)]
-    outs = [Outs(0), Outs(1)]
-    units = [Units(0), Units(1)]
+            self.units = [
+                Shared(layer, src, dst.at[layer, 1], mine, theirs, y_dev)
+                for src, dst in ((up_w, gup), (down_w, gdown))
+                for mine, theirs in halves(UNITS, 2)
+            ]
+
+        def everything(self):
+            return (
+                [self.heads_own, self.out_own, self.out_x] + self.small_own + self.units_own + self.heads + self.small
+                + self.out_y + self.units
+            )
+
+    layers = [Layer(0), Layer(1)]
+
+    def each(items, action):
+        for item in items:
+            getattr(item, action)()
+
     loads = {}
 
     def load_units(layer, when):
-        copies = [wires.local(gup.at[layer], uw), wires.local(gdown.at[layer], dw)]
-        for c in copies:
+        mine = [wires.local(up_w, uw.at[0]), wires.local(down_w, dw.at[0])]
+        sibs = [
+            wires.local(gup.at[layer, 0], uw.at[0], wires.locals - 2),
+            wires.local(gdown.at[layer, 0], dw.at[0], wires.locals - 1),
+        ]
+        rest = [wires.local(gup.at[layer, 1], uw.at[1]), wires.local(gdown.at[layer, 1], dw.at[1])]
+
+        @pl.when(core == layer)
+        def _():
+            for c in mine:
+                c.start()
+
+        @pl.when(core != layer)
+        def _():
+            for c in sibs:
+                c.start()
+
+        for c in rest:
             c.start()
-        loads[layer, when] = copies
+        loads[layer, when] = mine + rest
 
     def wait_units(layer, when):
         for c in loads[layer, when]:
@@ -475,8 +507,9 @@
     tokens = Tokens(states, xb.at[0])
     ends = Tokens(cotangent, cot)
 
+    first = layers[0]
     tokens.start()
-    heads[0].start()
+    each([first.heads_own] + first.small_own, "start")
     tokens.wait()
 
     def chunk_rows(step):
@@ -496,8 +529,13 @@
 
     for step in range(STEPS):
         gather_x(0, step)
-    units[0].start()
-    outs[0].start()
+
+    @pl.when(core == 0)
+    def _():
+        for step in range(STEPS):
+            gathers[0, step].wait_send()
+
+    each(first.heads + first.small, "start")
 
     parity = low + core - 2 * low * core
     row = segments[pl.ds(low, 1), :]
@@ -515,8 +553,8 @@
             lab_q[pl.ds(index * ROWS, ROWS), :] = same.astype(BF16)
         lab_k[pl.ds(index * ROWS, ROWS), :] = differ.astype(BF16)
 
-    def project(layer, source, start, size):
-        for slot in range(2):
+    def project(layer, source, start, size, slots=(0, 1)):
+        for slot in slots:
             columns = slice(slot * QUARTER, (slot + 1) * QUARTER)
             rows = pl.ds(start, size)
             qs[layer, rows, columns] = dot(source, qw[layer, slot, 0]).astype(BF16)
@@ -613,42 +651,58 @@
         scales[layer, rows, :] = jnp.broadcast_to(scale, (CHUNK, PAIR))
 
     def forward_attention(layer):
+        this, later = layers[layer], layers[1]
         if layer == 0:
-            heads[0].forward()
-        heads[layer].need()
-        project(layer, xb[layer], 0, ROWS)
-        sent = [send_chunk(kv.at[layer, :ROWS], kvs.at[layer, :ROWS], sib_dev)]
-        for step in range(STEPS):
-            gathers[layer, step].wait_recv()
-            project(layer, xg[chunk_rows(step), :], ROWS + step * CHUNK, CHUNK)
-        sent.append(send_chunk(kv.at[layer, ROWS:], kvs.at[layer, ROWS:], sib_dev))
-        if layer == 0:
-            heads[1].start()
-            outs[0].forward()
-            units[0].forward(0)
+            this.heads_own.need()
+            project(0, xb[0], 0, ROWS, (0,))
+            for step in range(STEPS):
+                gathers[0, step].wait_recv()
+                project(0, xg[chunk_rows(step), :], ROWS + step * CHUNK, CHUNK, (0,))
+            each(this.units, "start")
+            this.out_x.start()
+            each(this.heads, "forward")
+            each(this.small, "forward")
+            each(this.heads, "forward_last")
+            each([this.out_own] + this.units_own, "start")
+            each(this.heads + this.small_own + this.small, "need")
+            project(0, xb[0], 0, ROWS, (1,))
+            sent = [send_chunk(kv.at[0, :ROWS], kvs.at[0, :ROWS], sib_dev)]
+            project(0, xg[...], ROWS, ROWS, (1,))
+            sent.append(send_chunk(kv.at[0, ROWS:], kvs.at[0, ROWS:], sib_dev))
+            this.out_x.forward()
+            each(this.out_y, "start")
+            each(later.heads + later.small, "start")
+            each(this.units[:2], "forward")
+        else:
+            each([this.heads_own] + this.heads + this.small_own + this.small, "need")
+            project(1, xb[1], 0, ROWS)
+            sent = [send_chunk(kv.at[1, :ROWS], kvs.at[1, :ROWS], sib_dev)]
+            for step in range(STEPS):
+                gathers[1, step].wait_recv()
+                project(1, xg[chunk_rows(step), :], ROWS + step * CHUNK, CHUNK)
+            sent.append(send_chunk(kv.at[1, ROWS:], kvs.at[1, ROWS:], sib_dev))
+            each(this.out_y, "start")
         for c in sent:
             c.wait_recv()
         attend_rows(layer, ROWS)
         swap = send_chunk(mg.at[layer, ROWS:], mrecv, y_dev)
         if layer == 0:
-            outs[0].forward_last()
-            units[0].forward(1)
-            units[0].forward_last(0)
+            each(this.units[2:], "forward")
+            each(this.units[:2], "forward_last")
         else:
-            units[1].forward(1)
-            units[1].forward_last(0)
+            each(this.out_y, "forward")
+            each(this.units, "forward_last")
         attend_rows(layer, 0)
         if layer == 0:
-            outs[1].start()
+            each(this.out_y, "forward")
+            each(this.units[2:], "forward_last")
+            each(this.out_y, "forward_last")
             ends.start()
-            units[0].forward_last(1)
-            units[0].need()
-            load_units(0, 0)
         else:
-            units[1].forward_last(1)
-            units[1].need()
-            load_units(1, 0)
-        outs[layer].need()
+            each(this.out_y, "forward_last")
+        each(this.units_own + this.units, "need")
+        load_units(layer, 0)
+        each([this.out_own, this.out_x] + this.out_y, "need")
         swap.wait_recv()
         copies = []
         for step in range(STEPS):
@@ -663,8 +717,14 @@
             mid[rows, :] = middle
             fsnd[rows, :] = middle.astype(BF16)
             copies.append(send_chunk(fsnd.at[rows], fin.at[rows], x_dev))
-        for c in sent + [swap] + [gathers[layer, s] for s in range(STEPS)]:
+        for c in sent + [swap]:
             c.wait_send()
+
+        def gathered():
+            for step in range(STEPS):
+                gathers[layer, step].wait_send()
+
+        gathered() if layer == 1 else pl.when(core == 1)(gathered)
         return copies
 
     def feed_rows(layer, source, start, size):
@@ -777,12 +837,14 @@
 
     copies = forward_attention(0)
     wait_units(0, 0)
-    heads[1].forward()
-    units[1].start()
-    outs[1].forward()
+    second = layers[1]
+    each([second.heads_own] + second.small_own + [second.out_own] + second.units_own, "start")
+    each(second.units, "start")
+    second.out_x.start()
+    each(second.heads + second.small, "forward")
     feed(0, copies, False, forward_finish(0))
-    outs[1].forward_last()
-    units[1].forward(0)
+    second.out_x.forward()
+    each(second.units, "forward")
     copies = forward_attention(1)
     wait_units(1, 0)
     feed(1, copies, False, forward_finish(1))
@@ -924,10 +986,8 @@
         arrived()
     tokens.finish()
     ends.finish()
-    for layer in range(2):
-        heads[layer].finish()
-        outs[layer].finish()
-        units[layer].finish()
+    for layer in layers:
+        each(layer.everything(), "finish")
 
 
 def fused(dp, states, cotangent, segments, qkv, out_w, up_w, down_w, pre, pack):

time: 365 us -> 293 us (0.80)
  Pallas kernels: 358 us -> 286 us
    pallas_call x1, Pallas kernels: 358 us -> 286 us  [fused(): pl.pallas_call(functools.partial(fused_kernel, dp), out_shape=[shape((2,...]
where the time goes in v3:
time: 293 us
  Pallas kernels  286 us (98%)
  local copies, waits for them, and re-layouts  4.47 us (2%)
    pallas_call x1, Pallas kernels, fused(): pl.pallas_call(functools.partial(fused_kernel, dp), out_shape=[shape((2,...  286 us

profile of v3, /device:TPU:0, one launch (start us, length us, event | category | flops | bytes accessed | tf_op | source)
XLA Modules:
  0.0 293.0 jit_solution(3664264064109679557)
XLA Ops:
  0.6 0.1 pad.3.clone
  0.7 1.4 maximum_convert_fusion.pack
  2.1 286.5 %layers.1 = (bf16[2,256,1024]{2,1,0:T(8,128)(2,1)}, f32[2,256,1024]{2,1,0:T(8,128)}, f32[2,64,256]{2,1,0:T(8,128)}, bf16[2,2,1024,1024]{3,2,1,0:T(8,128)(2,1)}, bf16[2,2,1024,1024]{3,2,1,0:T(8,128)(2,1)}) custom-call(bf16[2,256,1024]{2,1,0:T(8,128)(2,1)} %states.1, bf16[2,256,1024]{2,1,0:T(8,128)(2,1)} %cotangent.1, s32[2,1024]{1,0:T(2,128)} %segments.1, ...), custom_call_target="tpu_custom_call" | custom-call | tf_op jit(solution)/shard_map/layers/pallas_call | solution.py:1028
  288.6 0.0 copy-start
  288.6 2.4 copy.17
  291.0 0.0 copy-done
  291.0 0.0 copy-start.1
  291.0 1.3 copy.18
  292.3 0.0 copy-done.1
  292.3 0.7 copy.19
Async XLA Ops:
  288.6 2.4 copy-start
  291.0 1.3 copy-start.1
